TPU v7x, 32 devices: a whole 2x2x4 slice. The times are simulated.
32 devices in a mesh: tp: 4 (over y, x), cp: 4 (over z), dp: 2 (over core).
Axes of the slice: x: 2, y: 2, z: 4, core: 2. Of those that a mesh axis runs over, the one named last changes fastest.
Arguments:
- tokens: bfloat16 [4096, 2, 768], P(('cp', 'tp'), 'dp'), may hold values from -6 to 6
- segment_ids: int32 [4096, 2], P('cp', 'dp'), may hold values from 0 to 2, as said below
- ln1_gain: float32 [768], replicated, may hold values from 0.5 to 1.5
- ln1_bias: float32 [768], replicated, may hold values from -1.75 to 1.75
- w_qkv: bfloat16 [768, 3, 768], P(None, None, 'tp'), may hold values from -0.21875 to 0.21875
- b_qkv: float32 [3, 768], P(None, 'tp'), may hold values from -1.75 to 1.75
- w_feat: bfloat16 [12, 64, 64], P('tp'), may hold values from -1.5 to 1.5
- b_feat: float32 [12, 64], P('tp'), may hold values from -3 to 3
- output_weight: bfloat16 [768, 768], P('tp'), may hold values from -3 to 3
- b_out: float32 [768], replicated, may hold values from -1.75 to 1.75
- ln2_gain: float32 [768], replicated, may hold values from 0.5 to 1.5
- ln2_bias: float32 [768], replicated, may hold values from -1.75 to 1.75
- w_up: bfloat16 [768, 3072], P(None, 'tp'), may hold values from -0.21875 to 0.21875
- b_up: float32 [3072], P('tp'), may hold values from -1.75 to 1.75
- w_down: bfloat16 [3072, 768], P('tp'), may hold values from -0.109375 to 0.109375
- b_down: float32 [768], replicated, may hold values from -1.75 to 1.75
- cotangent: bfloat16 [4096, 2, 768], P(('cp', 'tp'), 'dp'), may hold values from -6 to 6
Outputs:
- out_tokens: bfloat16 [4096, 2, 768], P(('cp', 'tp'), 'dp')
- d_tokens: float32 [4096, 2, 768], P(('cp', 'tp'), 'dp')
- d_ln1_gain: float32 [768], replicated
- d_ln1_bias: float32 [768], replicated
- d_w_qkv: float32 [768, 3, 768], P(None, None, 'tp')
- d_b_qkv: float32 [3, 768], P(None, 'tp')
- d_w_feat: float32 [12, 64, 64], P('tp')
- d_b_feat: float32 [12, 64], P('tp')
- d_w_out: float32 [768, 768], P('tp')
- d_b_out: float32 [768], replicated
- d_ln2_gain: float32 [768], replicated
- d_ln2_bias: float32 [768], replicated
- d_w_up: float32 [768, 3072], P(None, 'tp')
- d_b_up: float32 [3072], P('tp')
- d_w_down: float32 [3072, 768], P('tp')
- d_b_down: float32 [768], replicated
Inputs may be any that keep to these rules, and one draw needn't show every extreme that they name: `segment_ids`: in each packed row the ids start at 0 and never fall; they rise by one at one position of 1 to 1023 and again at one position of 3073 to 4095.
All inputs are finite; a program needn't handle non-finite values.
Results may differ from a plain program's by a relative error of at most 0.012.
The roundings to bfloat16 on the way count: a program that leaves them out, or rounds other values in their place, can miss the bound.
Values may be sent and summed in bfloat16 or wider, within the bound.
No kernel may reach another device: no remote copies, remote signals or barrier semaphores. Data moves between devices by JAX's collectives and lax.ppermute only.
A program may use at most 128 MiB of HBM per device.

v0:
```python
import jax
import jax.numpy as jnp
from jax import lax
from jax.sharding import PartitionSpec as P

FULL_PRECISION = lax.Precision.HIGHEST
epsilon = 1e-05


def prefix(value, axis, join, neutral, backward):
    count, mine = (lax.axis_size(axis), lax.axis_index(axis))
    pieces = jax.tree.map(lambda part: lax.all_gather(part, axis), value)
    if backward:
        pieces = jax.tree.map(lambda part: part[::-1], pieces)
        mine = count - 1 - mine
    total = jax.tree.map(
        lambda part, zero: jnp.full_like(part, 0) + jnp.asarray(zero, part.dtype), value, neutral
    )

    def turn(position, total):
        longer = join(total, jax.tree.map(lambda part: part[position], pieces))
        return jax.tree.map(lambda new, old: jnp.where(position < mine, new, old), longer, total)

    return lax.fori_loop(0, count - 1, turn, total)


def norm_rows(values, gain_vec, bias_vec):
    centred = values - jnp.mean(values, axis=-1, keepdims=True)
    variance = jnp.mean(centred * centred, axis=-1, keepdims=True)
    return centred * lax.rsqrt(variance + epsilon) * gain_vec + bias_vec


def norm_back(values, gain_vec, grad_out):
    centred = values - jnp.mean(values, axis=-1, keepdims=True)
    variance = jnp.mean(centred * centred, axis=-1, keepdims=True)
    inv_std = lax.rsqrt(variance + epsilon)
    x_hat = centred * inv_std
    grad_hat = grad_out * gain_vec
    grad_in = inv_std * (
        grad_hat
        - jnp.mean(grad_hat, axis=-1, keepdims=True)
        - x_hat * jnp.mean(grad_hat * x_hat, axis=-1, keepdims=True)
    )
    return (grad_in, grad_out * x_hat)


def feature_soft(logits):
    return jax.nn.softmax(jnp.concatenate([logits, -logits], axis=-1), axis=-1)


def join_segments(earlier_part, later_part):
    seg_now = jnp.where(later_part[0] < 0, earlier_part[0], later_part[0])
    keep_flag = (earlier_part[0] == seg_now).astype(jnp.float32)
    return (
        seg_now,
        later_part[1] + keep_flag[:, None, None, None] * earlier_part[1],
        later_part[2] + keep_flag[:, None, None] * earlier_part[2],
    )


def pass_on(carry, item):
    return (join_segments(carry, item), carry)


def shards(
    tokens,
    segment_ids,
    ln1_gain,
    ln1_bias,
    w_qkv,
    b_qkv,
    w_feat,
    b_feat,
    output_weight,
    b_out,
    ln2_gain,
    ln2_bias,
    w_up,
    b_up,
    w_down,
    b_down,
    cotangent,
):
    single_float = jnp.float32
    bf16 = jnp.bfloat16
    local_rows = tokens.shape[0]
    full_rows = local_rows * lax.axis_size("tp")
    batch_rows = tokens.shape[1]
    head_local = w_feat.shape[0]
    head_dim = w_feat.shape[1]
    feat_dim = 2 * head_dim
    seg_float = segment_ids.astype(single_float)

    def widen_rows(rounded):
        return lax.all_gather(rounded, "tp", axis=0, tiled=True)

    def reduce_rows(term_fn):
        return lax.psum_scatter(
            term_fn(jnp.int32(0), local_rows * lax.axis_size("tp")),
            "tp",
            scatter_dimension=0,
            tiled=True,
        )

    def reduce_grads(term_fn):
        return lax.psum_scatter(
            term_fn(jnp.int32(0), local_rows * lax.axis_size("tp")),
            "tp",
            scatter_dimension=0,
            tiled=True,
        )

    start_rows = tokens.astype(single_float)
    normed_one = norm_rows(start_rows, ln1_gain, ln1_bias)
    normed_low = widen_rows(normed_one.astype(bf16))
    projected = (
        jnp.einsum("tbd,dcm->tbcm", normed_low, w_qkv, preferred_element_type=single_float) + b_qkv
    )
    proj_low = projected.astype(bf16)
    heads_view = proj_low.reshape(full_rows, batch_rows, 3, head_local, head_dim)
    query_in = heads_view[:, :, 0]
    key_in = heads_view[:, :, 1]
    value_in = heads_view[:, :, 2]
    query_logit = (
        jnp.einsum("tbhd,hde->tbhe", query_in, w_feat, preferred_element_type=single_float) + b_feat
    )
    key_logit = (
        jnp.einsum("tbhd,hde->tbhe", key_in, w_feat, preferred_element_type=single_float) + b_feat
    )
    query_soft, query_pull = jax.vjp(feature_soft, query_logit)
    key_soft, key_pull = jax.vjp(feature_soft, key_logit)
    query_feat = query_soft.astype(bf16)
    key_features_mapped = key_soft.astype(bf16)
    last_seg = segment_ids[-1]
    last_mask = (segment_ids == last_seg[None, :]).astype(bf16)
    masked_keys = key_features_mapped * last_mask[:, :, None, None]
    state_local = jnp.einsum(
        "tbhf,tbhd->bhfd", masked_keys, value_in, preferred_element_type=single_float
    )
    norm_local = jnp.sum(masked_keys, axis=0, dtype=single_float)
    empty_state = (
        -jnp.ones((batch_rows,), single_float),
        jnp.zeros((batch_rows, head_local, feat_dim, head_dim), single_float),
        jnp.zeros((batch_rows, head_local, feat_dim), single_float),
    )
    carry_seg, carry_state, carry_norm = prefix(
        (last_seg.astype(single_float), state_local, norm_local),
        "cp",
        join_segments,
        empty_state,
        False,
    )
    use_carry = (seg_float == carry_seg[None, :]).astype(single_float)
    group_len = min(64, full_rows)
    group_count = full_rows // group_len

    def grouped(values):
        return values.reshape((group_count, group_len) + values.shape[1:])

    q_groups = grouped(query_feat)
    k_groups = grouped(key_features_mapped)
    v_groups = grouped(value_in)
    seg_groups = grouped(segment_ids)
    seg_groups_float = seg_groups.astype(single_float)
    q_groups_wide = q_groups.astype(single_float)
    k_groups_wide = k_groups.astype(single_float)
    v_groups_wide = v_groups.astype(single_float)
    inner_pos = jnp.arange(group_len, dtype=jnp.int32)
    causal = inner_pos[None, :] <= inner_pos[:, None]
    seg_by_row = jnp.transpose(seg_groups, (0, 2, 1))
    same_doc = seg_by_row[:, :, :, None] == seg_by_row[:, :, None, :]
    pair_mask = (causal[None, None] & same_doc).astype(single_float)[:, :, None]
    attention_scores = jnp.einsum(
        "nqbhf,nkbhf->nbhqk", q_groups, k_groups, preferred_element_type=single_float
    )
    weights = attention_scores * pair_mask
    numer_inner = jnp.einsum("nbhqk,nkbhd->nqbhd", weights, v_groups_wide, precision=FULL_PRECISION)
    denom_inner = jnp.transpose(jnp.sum(weights, axis=-1), (0, 3, 1, 2))
    seg_tail = seg_groups[:, -1]
    tail_mask = (seg_groups == seg_tail[:, None]).astype(bf16)[..., None, None]
    tail_keys = k_groups * tail_mask
    tail_state = jnp.einsum(
        "ncbhf,ncbhd->nbhfd", tail_keys, v_groups, preferred_element_type=single_float
    )
    tail_norm = jnp.sum(tail_keys, axis=1, dtype=single_float)
    _, (seg_in, state_in, norm_in) = lax.scan(
        pass_on, empty_state, (seg_tail.astype(single_float), tail_state, tail_norm)
    )
    use_in = (seg_groups_float == seg_in[:, None]).astype(single_float)[..., None]
    use_cp = grouped(use_carry)[..., None]
    numer_groups = (
        numer_inner
        + use_in[..., None]
        * jnp.einsum("nqbhf,nbhfd->nqbhd", q_groups_wide, state_in, precision=FULL_PRECISION)
        + use_cp[..., None]
        * jnp.einsum("nqbhf,bhfd->nqbhd", q_groups_wide, carry_state, precision=FULL_PRECISION)
    )
    denom_groups = (
        denom_inner
        + use_in * jnp.einsum("nqbhf,nbhf->nqbh", q_groups_wide, norm_in, precision=FULL_PRECISION)
        + use_cp
        * jnp.einsum("nqbhf,bhf->nqbh", q_groups_wide, carry_norm, precision=FULL_PRECISION)
    )
    numerator_all = numer_groups.reshape(full_rows, batch_rows, head_local, head_dim)
    denominator_all = denom_groups.reshape(full_rows, batch_rows, head_local)
    attn_out = numerator_all / denominator_all[..., None]
    attention_reduced = attn_out.astype(bf16).reshape(full_rows, batch_rows, head_local * head_dim)

    def out_terms(row_start, row_count):
        return jnp.einsum(
            "rsw,wc->rsc", attention_reduced, output_weight, preferred_element_type=single_float
        )

    middle = start_rows + (reduce_rows(out_terms) + b_out)
    normed_two = norm_rows(middle, ln2_gain, ln2_bias)
    normed_two_low = widen_rows(normed_two.astype(bf16))
    hidden_pre = (
        jnp.einsum("tbd,df->tbf", normed_two_low, w_up, preferred_element_type=single_float) + b_up
    )
    hidden_low = jax.nn.gelu(hidden_pre, approximate=True).astype(bf16)

    def down_terms(row_start, row_count):
        return jnp.einsum("tbf,fd->tbd", hidden_low, w_down, preferred_element_type=single_float)

    block_out = middle + reduce_rows(down_terms) + b_down
    out_tokens = block_out.astype(bf16)
    cot_full = widen_rows(cotangent)
    grad_w_down = jnp.einsum(
        "tbf,tbd->fd", hidden_low, cot_full, preferred_element_type=single_float
    )
    grad_hidden = jnp.einsum("tbd,fd->tbf", cot_full, w_down, preferred_element_type=single_float)
    gelu_pull = jax.vjp(lambda pre_act: jax.nn.gelu(pre_act, approximate=True), hidden_pre)[1]
    grad_pre_low = gelu_pull(grad_hidden)[0].astype(bf16)
    grad_w_up = jnp.einsum(
        "tbd,tbf->df", normed_two_low, grad_pre_low, preferred_element_type=single_float
    )
    grad_b_up = jnp.sum(grad_pre_low, axis=(0, 1), dtype=single_float)

    def up_back_terms(row_start, row_count):
        return jnp.einsum("tbf,df->tbd", grad_pre_low, w_up, preferred_element_type=single_float)

    grad_normed_two = reduce_grads(up_back_terms)
    grad_middle_ln, gain_two_rows = norm_back(middle, ln2_gain, grad_normed_two)
    grad_middle = cotangent.astype(single_float) + grad_middle_ln
    grad_middle_low = grad_middle.astype(bf16)
    branch_gradient_complete = widen_rows(grad_middle_low)
    output_weight_gradient = jnp.einsum(
        "zkc,zka->ca",
        attention_reduced,
        branch_gradient_complete,
        preferred_element_type=single_float,
    )
    attention_gradient = jnp.einsum(
        "hjy,ky->hjk", branch_gradient_complete, output_weight, preferred_element_type=single_float
    )
    attention_gradient = (
        attention_gradient.astype(bf16)
        .astype(single_float)
        .reshape(full_rows, batch_rows, head_local, head_dim)
    )
    grad_num = attention_gradient / denominator_all[..., None]
    grad_den = -jnp.sum(attention_gradient * attn_out, axis=-1) / denominator_all
    first_seg = segment_ids[0]
    first_mask = (segment_ids == first_seg[None, :]).astype(single_float)[:, :, None, None]
    query_wide = query_feat.astype(single_float)
    state_grad_local = jnp.einsum(
        "tbhf,tbhd->bhfd", query_wide * first_mask, grad_num, precision=FULL_PRECISION
    )
    norm_grad_local = jnp.einsum(
        "tbhf,tbh->bhf", query_wide * first_mask, grad_den, precision=FULL_PRECISION
    )
    coming = prefix(
        (first_seg.astype(single_float), state_grad_local, norm_grad_local),
        "cp",
        join_segments,
        empty_state,
        True,
    )
    takes_grad = (coming[0] == last_seg.astype(single_float)).astype(single_float)
    state_grad_out = takes_grad[:, None, None, None] * coming[1]
    norm_grad_out = takes_grad[:, None, None] * coming[2]
    gnum_groups = grouped(grad_num)
    gden_groups = grouped(grad_den)
    grad_weights = (
        jnp.einsum("nqbhd,nkbhd->nbhqk", gnum_groups, v_groups_wide, precision=FULL_PRECISION)
        + jnp.transpose(gden_groups, (0, 2, 3, 1))[..., None]
    ) * pair_mask
    grad_q_groups = (
        jnp.einsum("nbhqk,nkbhf->nqbhf", grad_weights, k_groups_wide, precision=FULL_PRECISION)
        + use_in[..., None]
        * (
            jnp.einsum("nqbhd,nbhfd->nqbhf", gnum_groups, state_in, precision=FULL_PRECISION)
            + gden_groups[..., None] * norm_in[:, None]
        )
        + use_cp[..., None]
        * (
            jnp.einsum("nqbhd,bhfd->nqbhf", gnum_groups, carry_state, precision=FULL_PRECISION)
            + gden_groups[..., None] * carry_norm[None, None]
        )
    )
    grad_k_inner = jnp.einsum(
        "nbhqk,nqbhf->nkbhf", grad_weights, q_groups_wide, precision=FULL_PRECISION
    )
    grad_v_inner = jnp.einsum("nbhqk,nqbhd->nkbhd", weights, gnum_groups, precision=FULL_PRECISION)
    seg_head = seg_groups[:, 0]
    head_mask = (seg_groups == seg_head[:, None]).astype(single_float)[..., None, None]
    head_queries = q_groups_wide * head_mask
    head_state = jnp.einsum(
        "ncbhf,ncbhd->nbhfd", head_queries, gnum_groups, precision=FULL_PRECISION
    )
    head_norm = jnp.einsum("ncbhf,ncbh->nbhf", head_queries, gden_groups, precision=FULL_PRECISION)
    _, (seg_out, gstate_out, gnorm_out) = lax.scan(
        pass_on, empty_state, (seg_head.astype(single_float), head_state, head_norm), reverse=True
    )
    reach = (seg_groups_float == seg_out[:, None]).astype(single_float)[..., None, None]
    grad_k_groups = grad_k_inner + reach * (
        jnp.einsum("nkbhd,nbhfd->nkbhf", v_groups_wide, gstate_out, precision=FULL_PRECISION)
        + gnorm_out[:, None]
    )
    grad_v_groups = grad_v_inner + reach * jnp.einsum(
        "nkbhf,nbhfd->nkbhd", k_groups_wide, gstate_out, precision=FULL_PRECISION
    )
    grad_query = grad_q_groups.reshape(full_rows, batch_rows, head_local, feat_dim)
    grad_key = grad_k_groups.reshape(full_rows, batch_rows, head_local, feat_dim)
    grad_value = grad_v_groups.reshape(full_rows, batch_rows, head_local, head_dim)
    value_wide = v_groups_wide.reshape(full_rows, batch_rows, head_local, head_dim)
    key_wide = k_groups_wide.reshape(full_rows, batch_rows, head_local, feat_dim)
    last_wide = last_mask.astype(single_float)[:, :, None, None]
    grad_key = grad_key + last_wide * (
        jnp.einsum("tbhd,bhfd->tbhf", value_wide, state_grad_out, precision=FULL_PRECISION)
        + norm_grad_out[None]
    )
    grad_value = grad_value + last_wide * jnp.einsum(
        "tbhf,bhfd->tbhd", key_wide, state_grad_out, precision=FULL_PRECISION
    )
    grad_q_logit = query_pull(grad_query)[0]
    grad_k_logit = key_pull(grad_key)[0]
    feat_wide = w_feat.astype(single_float)
    grad_q_in = jnp.einsum("tbhe,hde->tbhd", grad_q_logit, feat_wide, precision=FULL_PRECISION)
    grad_k_in = jnp.einsum("tbhe,hde->tbhd", grad_k_logit, feat_wide, precision=FULL_PRECISION)
    grad_w_feat = jnp.einsum(
        "tbhd,tbhe->hde", query_in.astype(single_float), grad_q_logit, precision=FULL_PRECISION
    ) + jnp.einsum(
        "tbhd,tbhe->hde", key_in.astype(single_float), grad_k_logit, precision=FULL_PRECISION
    )
    grad_b_feat = jnp.sum(grad_q_logit + grad_k_logit, axis=(0, 1))
    grad_proj = jnp.stack([grad_q_in, grad_k_in, grad_value], axis=2)
    grad_proj = grad_proj.reshape(full_rows, batch_rows, 3, head_local * head_dim).astype(bf16)
    grad_w_qkv = jnp.einsum(
        "tbd,tbcm->dcm", normed_low, grad_proj, preferred_element_type=single_float
    )
    grad_b_qkv = jnp.sum(grad_proj, axis=(0, 1), dtype=single_float)

    def qkv_back_terms(row_start, row_count):
        return jnp.einsum("tbcm,dcm->tbd", grad_proj, w_qkv, preferred_element_type=single_float)

    grad_normed_one = reduce_grads(qkv_back_terms)
    grad_start_ln, gain_one_rows = norm_back(start_rows, ln1_gain, grad_normed_one)
    grad_tokens = grad_middle + grad_start_ln
    row_grads = lax.psum(
        (
            jnp.sum(gain_one_rows, axis=(0, 1)),
            jnp.sum(grad_normed_one, axis=(0, 1)),
            jnp.sum(grad_middle_low, axis=(0, 1), dtype=single_float),
            jnp.sum(gain_two_rows, axis=(0, 1)),
            jnp.sum(grad_normed_two, axis=(0, 1)),
            jnp.sum(cotangent, axis=(0, 1), dtype=single_float),
        ),
        ("tp", "cp", "dp"),
    )
    (
        grad_w_qkv,
        grad_b_qkv,
        grad_w_feat,
        grad_b_feat,
        output_weight_gradient,
        grad_w_up,
        grad_b_up,
        grad_w_down,
    ) = lax.psum(
        (
            grad_w_qkv,
            grad_b_qkv,
            grad_w_feat,
            grad_b_feat,
            output_weight_gradient,
            grad_w_up,
            grad_b_up,
            grad_w_down,
        ),
        ("cp", "dp"),
    )
    return (
        out_tokens,
        grad_tokens,
        row_grads[0],
        row_grads[1],
        grad_w_qkv,
        grad_b_qkv,
        grad_w_feat,
        grad_b_feat,
        output_weight_gradient,
        row_grads[2],
        row_grads[3],
        row_grads[4],
        grad_w_up,
        grad_b_up,
        grad_w_down,
        row_grads[5],
    )


def solution(mesh):
    placed = (
        P(("cp", "tp"), "dp", None),
        P("cp", "dp"),
        P(),
        P(),
        P(None, None, "tp"),
        P(None, "tp"),
        P("tp", None, None),
        P("tp", None),
        P("tp", None),
        P(),
        P(),
        P(),
        P(None, "tp"),
        P("tp"),
        P("tp", None),
        P(),
        P(("cp", "tp"), "dp", None),
    )
    return jax.shard_map(
        shards,
        mesh=mesh,
        in_specs=placed,
        out_specs=(
            P(("cp", "tp"), "dp", None),
            P(("cp", "tp"), "dp", None),
            P(),
            P(),
            P(None, None, "tp"),
            P(None, "tp"),
            P("tp", None, None),
            P("tp", None),
            P("tp", None),
            P(),
            P(),
            P(),
            P(None, "tp"),
            P("tp"),
            P("tp", None),
            P(),
        ),
        check_vma=False,
    )
```

profile of v0, /device:TPU:0, one launch (start us, length us, event | category | flops | bytes accessed | tf_op | source)
XLA Modules:
  0.0 988.3 jit_solution(11967611658393201010)
XLA Ops:
  15.8 14.0 %all-reduce.5 = (f32[4]{0:T(128)}, f32[4]{0:T(128)}) all-reduce(f32[4]{0:T(128)S(1)} %bitcast_dynamic-update-slice_fusion.5, f32[4]{0:T(128)S(1)} %bitcast_dynamic-update-slice_fusion.4), channel_id=1, replica_groups=mesh['tp'=4,'cp'=4,'dp'=2] {'cp'}, use_global_device_ids=true, to_apply=%add | all-reduce | flops 8 | bytes 64
  34.8 10.9 %all-gather.11.cloned.1.call-done = bf16[1024,1,768]{2,0,1:T(8,128)(2,1)} async-done(((bf16[256,1,768]{2,0,1:T(8,128)(2,1)}), bf16[1024,1,768]{2,0,1:T(8,128)(2,1)}) %all-gather.11.cloned.1.call-update) | async-done | bytes 1572880 | tf_op jit(solution)/shard_map/all_gather | solution.py:95
  45.7 2.5 fusion.62
  53.3 2.2 fusion.147
  60.5 2.6 concatenate.122
  68.5 2.4 reshape.1332
  70.9 2.7 copy.295
  73.5 3.2 copy.269
  76.7 3.2 copy.274
  82.4 11.9 %all-gather.4 = f32[4,3,128]{2,1,0:T(4,128)S(1)} all-gather(f32[1,3,128]{2,1,0:T(4,128)S(1)} %bitcast.580), channel_id=3, replica_groups=mesh['tp'=4,'cp'=4,'dp'=2] {'cp'}, dimensions={0}, use_global_device_ids=true | all-gather | bytes 7680 | tf_op jit(solution)/shard_map/all_gather | solution.py:12
  102.4 27.7 %all-gather = f32[12,128,64]{1,2,0:T(8,128)} all-gather(f32[3,128,64]{1,2,0:T(8,128)S(1)} %fusion.117), channel_id=2, replica_groups=mesh['tp'=4,'cp'=4,'dp'=2] {'cp'}, dimensions={0}, use_global_device_ids=true | all-gather | bytes 491520 | tf_op jit(solution)/shard_map/all_gather | solution.py:12
  130.0 9.3 while.89
  140.1 3.2 copy.270
  143.3 2.8 convert_reduce_fusion.1
  146.3 3.2 copy.275
  149.4 2.8 fusion.70
  156.2 61.5 %while.88 = (s32[]{:T(128)}, f32[1]{0:T(128)}, f32[1,3,128,64]{3,2,1,0:T(8,128)S(1)}, f32[1,3,128]{2,1,0:T(4,128)S(1)}, f32[16,1]{0,1:T(1,128)S(1)}, /*index=5*/...) while((s32[]{:T(128)}, f32[1]{0:T(128)}, ...), condition=%wide.region_10.11_spmd.clone, body=%wide.region_9.10_spmd.clone.sunk | while | flops 99847 | bytes 991982 | solution.py:186
  218.4 2.9 fusion.71
  224.6 3.9 fusion.19
  233.0 2.9 fusion.161
  235.9 3.4 divide_convert_fusion
  241.3 2.6 reshape.1339
  245.2 3.2 convolution_bitcast_fusion.3
  248.5 42.3 %reduce-scatter.5.cloned.1.call-done = f32[256,1,768]{2,0,1:T(8,128)} async-done(((f32[1024,1,768]{2,0,1:T(8,128)}), f32[256,1,768]{2,0,1:T(8,128)}) %reduce-scatter.5.cloned.1.call-update) | async-done | bytes 786448 | tf_op jit(solution)/shard_map/reduce_scatter | solution.py:98
  295.3 30.5 %all-gather.13.cloned.1.call-done = bf16[1024,1,768]{2,0,1:T(8,128)(2,1)} async-done(((bf16[256,1,768]{2,0,1:T(8,128)(2,1)}), bf16[1024,1,768]{2,0,1:T(8,128)(2,1)}) %all-gather.13.cloned.1.call-update) | async-done | bytes 1572880 | tf_op jit(solution)/shard_map/all_gather | solution.py:95
  325.8 4.8 fusion.57
  330.5 27.9 %all-gather.15.cloned.1.call-done = bf16[1024,1,768]{2,0,1:T(8,128)(2,1)} async-done(((bf16[256,1,768]{2,0,1:T(8,128)(2,1)}), bf16[1024,1,768]{2,0,1:T(8,128)(2,1)}) %all-gather.15.cloned.1.call-update) | async-done | bytes 1572880 | tf_op jit(solution)/shard_map/all_gather | solution.py:95
  358.5 6.5 convert_reduce_fusion
  366.2 3.1 convolution_bitcast_fusion.1
  369.4 5.7 convolution_bitcast_fusion.2
  375.2 38.3 %reduce-scatter.9.cloned.1.call-done = f32[256,1,768]{2,0,1:T(8,128)} async-done(((f32[1024,1,768]{2,0,1:T(8,128)}), f32[256,1,768]{2,0,1:T(8,128)}) %reduce-scatter.9.cloned.1.call-update) | async-done | bytes 786448 | tf_op jit(solution)/shard_map/reduce_scatter | solution.py:106
  413.4 2.1 multiply_reduce_fusion.1
  416.7 43.5 %reduce-scatter.7.cloned.1.call-done = f32[256,1,768]{2,0,1:T(8,128)} async-done(((f32[1024,1,768]{2,0,1:T(8,128)}), f32[256,1,768]{2,0,1:T(8,128)}) %reduce-scatter.7.cloned.1.call-update) | async-done | bytes 786448 | tf_op jit(solution)/shard_map/reduce_scatter | solution.py:98
  460.3 3.6 convert_reduce_fusion.6
  473.0 3.1 reshape.1347
  476.1 3.2 copy.309
  479.9 3.2 copy.310
  485.0 10.1 %all-gather.17.cloned.1.call-done = bf16[1024,1,768]{2,0,1:T(8,128)(2,1)} async-done(((bf16[256,1,768]{2,0,1:T(8,128)(2,1)}), bf16[1024,1,768]{2,0,1:T(8,128)(2,1)}) %all-gather.17.cloned.1.call-update) | async-done | bytes 1572880 | tf_op jit(solution)/shard_map/all_gather | solution.py:95
  505.1 2.9 fusion.74
  511.3 156.0 %while.90 = (s32[]{:T(128)}, f32[1]{0:T(128)}, f32[1,3,128,64]{3,2,1,0:T(8,128)S(1)}, f32[1,3,128]{2,1,0:T(4,128)}, f32[16,1]{0,1:T(1,128)}, /*index=5*/f32[16,1...) while((s32[]{:T(128)}, f32[1]{0:T(128)}, ...), condition=%wide.region_25.26_spmd.clone, body=%wide.region_24.25_spmd.clone.sunk | while | flops 99848 | bytes 992002 | solution.py:312
  667.4 6.7 fusion.15
  674.1 3.9 fusion.13
  679.6 2.6 fusion.64
  682.2 3.3 fusion.65
  685.5 11.9 %all-gather.5 = f32[4,3,128]{2,1,0:T(4,128)S(1)} all-gather(f32[1,3,128]{2,1,0:T(4,128)S(1)} %bitcast.581), channel_id=5, replica_groups=mesh['tp'=4,'cp'=4,'dp'=2] {'cp'}, dimensions={0}, use_global_device_ids=true | all-gather | bytes 7680 | tf_op jit(solution)/shard_map/all_gather | solution.py:12
  698.1 16.0 %all-gather.2 = f32[12,128,64]{1,2,0:T(8,128)} all-gather(f32[3,128,64]{1,2,0:T(8,128)S(1)} %fusion.65), channel_id=4, replica_groups=mesh['tp'=4,'cp'=4,'dp'=2] {'cp'}, dimensions={0}, use_global_device_ids=true | all-gather | bytes 491520 | tf_op jit(solution)/shard_map/all_gather | solution.py:12
  714.1 2.1 copy.319
  718.3 9.2 while.91
  727.6 2.4 add_multiply_fusion.2
  730.8 2.6 fusion.162
  733.4 3.8 fusion.40
  740.3 3.1 copy.322
  743.5 4.0 multiply_reduce_fusion
  749.5 3.0 reshape.1356
  752.6 2.9 fusion.80
  759.7 6.7 fusion.32
  771.5 3.1 convolution_bitcast_fusion
  777.6 4.9 fusion.55
  782.5 3.3 fusion.49
  788.8 2.3 fusion.60
  795.9 27.9 %all-reduce.3 = (f32[3,192]{1,0:T(4,128)}, f32[3,64,64]{2,1,0:T(8,128)}, f32[3,64]{1,0:T(4,128)}, f32[768]{0:T(1024)}) all-reduce(f32[3,192]{1,0:T(4,128)S(1)} %convert_reduce_fusion.2, f32[3,64,64]{2,1,0:T(8,128)S(1)} %convolution_add_fusion, f32[3,64]{1,0:T(4,128)} %add_reduce_fusion, ...), channel_id=1, replica_groups=mesh['tp'=4,'cp'=4,'dp'=2] {'cp','dp'}, use_global_device_ids=true, to_apply=%region_38.39 | all-reduce | flops 13824 | bytes 110592 | tf_op jit(solution)/shard_map/psum | solution.py:380
  827.5 39.0 %all-reduce.2 = (f32[768]{0:T(1024)}, f32[768]{0:T(1024)}, f32[768]{0:T(1024)}, f32[768]{0:T(1024)}, f32[768]{0:T(1024)}, /*index=5*/f32[768]{0:T(1024)}) all-reduce(f32[768]{0:T(1024)S(1)} %get-tuple-element.930, f32[768]{0:T(1024)S(1)} %get-tuple-element.935, ...), channel_id=1, replica_groups=mesh['tp'=4,'cp'=4,'dp'=2] {'tp','cp','dp'}, use_global_device_ids=true, to_apply=%region_33.34 | all-reduce | flops 4608 | bytes 36864 | tf_op jit(solution)/shard_map/psum | solution.py:360
  866.6 107.3 %all-reduce.8.cloned.1.call-done = (f32[768,3,192]{0,2,1:T(8,128)}, f32[192,768]{1,0:T(8,128)}, f32[768,768]{1,0:T(8,128)}, f32[768,768]{1,0:T(8,128)}) async-done(((f32[768,3,192]{0,2,1:T(8,128)}, f32[192,768]{1,0:T(8,128)}, f32[768,768]{1,0:T(8,128)}, f32[768,768]{1,0:T(8,128)}), (f32[768,3,192]{0,2,1:T(8,128)}, f32[192,768]{1,0:T(8,128)}, f32[768,768]{1,0:T(8,128)}, ...) | async-done | bytes 7077904 | tf_op jit(solution)/shard_map/psum | solution.py:380
  973.9 2.9 copy.475
  (716 shorter events, 309.6 us)
Async XLA Ops:
  7.2 351.3 %copy-start = (bf16[768,768]{1,0:T(8,128)(2,1)S(1)}, bf16[768,768]{1,0:T(8,128)(2,1)}, u32[]{:S(2)}) copy-start(bf16[768,768]{1,0:T(8,128)(2,1)} %param.39) | copy-start | bytes 3538948
  7.2 6.7 copy-start.137
  7.2 4.7 copy-start.91
  7.2 38.5 %copy-start.131 = (bf16[768,3,192]{0,2,1:T(8,128)(2,1)S(1)}, bf16[768,3,192]{0,2,1:T(8,128)(2,1)}, u32[]{:S(2)}) copy-start(bf16[768,3,192]{0,2,1:T(8,128)(2,1)} %param.29) | copy-start | bytes 2654212
  7.2 38.5 %all-gather.11.cloned.1.call-start = ((), (), s32[]{:S(2)}) async-start(), calls=%async_computation.4 | async-start | bytes 1966080 | tf_op jit(solution)/shard_map/all_gather | solution.py:95
  8.5 21.8 %copy-start.111 = (f32[256]{0:T(256)}, f32[256]{0:T(256)S(1)}, u32[]{:S(2)}) copy-start(f32[256]{0:T(256)S(1)} %broadcast_multiply_fusion.5) | copy-start | bytes 3076
  9.8 20.5 %copy-start.115 = (f32[256]{0:T(256)}, f32[256]{0:T(256)S(1)}, u32[]{:S(2)}) copy-start(f32[256]{0:T(256)S(1)} %add_rsqrt_fusion.1) | copy-start | bytes 3076
  11.9 278.9 %reduce-scatter.5.cloned.1.call-start = ((), (), s32[]{:S(2)}) async-start(), calls=%async_computation.5 | async-start | bytes 3932160 | tf_op jit(solution)/shard_map/reduce_scatter | solution.py:98
  31.1 17.2 %copy-start.74 = (s32[16,64]{1,0:T(8,128)}, s32[16,64]{1,0:T(8,128)S(1)}, u32[]{:S(2)}) copy-start(s32[16,64]{1,0:T(8,128)S(1)} %eq.144) | copy-start | bytes 12292
  31.3 17.0 %copy-start.127 = (s32[16,1,1]{0,2,1:T(1,128)}, s32[16,1,1]{0,2,1:T(1,128)S(1)}, u32[]{:S(2)}) copy-start(s32[16,1,1]{0,2,1:T(1,128)S(1)} %copy.364) | copy-start | bytes 196
  50.0 433.8 %copy-start.2 = (f32[3,64,1024,1]{2,1,0,3:T(8,128)}, f32[3,64,1024,1]{2,1,0,3:T(8,128)S(1)}, u32[]{:S(2)}) copy-start(f32[3,64,1024,1]{2,1,0,3:T(8,128)S(1)} %fusion.78) | copy-start | bytes 2359300
  55.5 25.8 %copy-start.4 = (f32[1024,1,3,64]{0,3,2,1:T(8,128)}, f32[1024,1,3,64]{0,3,2,1:T(8,128)S(1)}, u32[]{:S(2)}) copy-start(f32[1024,1,3,64]{0,3,2,1:T(8,128)S(1)} %get-tuple-element.1065) | copy-start | bytes 2359300
  57.8 5.3 copy-start.70
  82.4 18.5 %copy-start.114 = (bf16[1024]{0:T(1024)(128)(2,1)S(1)}, bf16[1024]{0:T(1024)(128)(2,1)}, u32[]{:S(2)}) copy-start(bf16[1024]{0:T(1024)(128)(2,1)} %fusion.142) | copy-start | bytes 6148
  95.1 7.2 copy-start.82
  100.9 29.1 %copy-start.26 = (f32[1,3,128,64]{3,2,1,0:T(8,128)S(1)}, f32[1,3,128,64]{3,2,1,0:T(8,128)}, u32[]{:S(2)}) copy-start(f32[1,3,128,64]{3,2,1,0:T(8,128)} %custom-call.2) | copy-start | bytes 294916
  100.9 29.1 %copy-start.94 = (f32[1,3,128]{2,1,0:T(4,128)S(1)}, f32[1,3,128]{2,1,0:T(4,128)}, u32[]{:S(2)}) copy-start(f32[1,3,128]{2,1,0:T(4,128)} %custom-call.3) | copy-start | bytes 4612
  100.9 29.1 %copy-start.136 = (f32[4]{0:T(128)S(1)}, f32[4]{0:T(128)}, u32[]{:S(2)}) copy-start(f32[4]{0:T(128)} %get-tuple-element.1026) | copy-start | bytes 52
  130.0 9.4 copy-start.92
  139.4 3.9 copy-start.27
  139.4 3.9 copy-start.95
  156.2 62.1 %copy-start.75 = (s32[16,64]{1,0:T(8,128)S(1)}, s32[16,64]{1,0:T(8,128)}, u32[]{:S(2)}) copy-start(s32[16,64]{1,0:T(8,128)} %copy-done.74) | copy-start | bytes 12292
  218.4 11.9 %copy-start.102 = (f32[16,64]{1,0:T(8,128)}, f32[16,64]{1,0:T(8,128)S(1)}, u32[]{:S(2)}) copy-start(f32[16,64]{1,0:T(8,128)S(1)} %fusion.140) | copy-start | bytes 12292
  218.4 4.9 copy-start.87
  218.4 6.2 copy-start.7
  221.3 279.6 %copy-start.9 = (bf16[16,64,3,128]{3,1,2,0:T(8,128)(2,1)}, bf16[16,64,3,128]{3,1,2,0:T(8,128)(2,1)S(1)}, u32[]{:S(2)}) copy-start(bf16[16,64,3,128]{3,1,2,0:T(8,128)(2,1)S(1)} %fusion.71) | copy-start | bytes 2359300
  224.6 3.9 copy-start.18
  224.6 3.9 copy-start.42
  248.4 77.4 %all-gather.13.cloned.1.call-start = ((), (), s32[]{:S(2)}) async-start(), calls=%async_computation.6 | async-start | bytes 1966080 | tf_op jit(solution)/shard_map/all_gather | solution.py:95
  294.7 63.8 %all-gather.15.cloned.1.call-start = ((), (), s32[]{:S(2)}) async-start(), calls=%async_computation.8 | async-start | bytes 1966080 | tf_op jit(solution)/shard_map/all_gather | solution.py:95
  295.3 118.2 %reduce-scatter.9.cloned.1.call-start = ((), (), s32[]{:S(2)}) async-start(), calls=%async_computation.9 | async-start | bytes 3932160 | tf_op jit(solution)/shard_map/reduce_scatter | solution.py:106
  358.5 7.7 copy-start.130
  369.3 90.9 %reduce-scatter.7.cloned.1.call-start = ((), (), s32[]{:S(2)}) async-start(), calls=%async_computation.7 | async-start | bytes 3932160 | tf_op jit(solution)/shard_map/reduce_scatter | solution.py:98
  375.1 38.4 %copy-start.12 = (f32[256,1,768]{2,0,1:T(8,128)S(1)}, f32[256,1,768]{2,0,1:T(8,128)}, u32[]{:S(2)}) copy-start(f32[256,1,768]{2,0,1:T(8,128)} %copy-done.11) | copy-start | bytes 2359300
  375.1 85.1 %copy-start.56 = (bf16[256,1,768]{2,0,1:T(8,128)(2,1)S(1)}, bf16[256,1,768]{2,0,1:T(8,128)(2,1)}, u32[]{:S(2)}) copy-start(bf16[256,1,768]{2,0,1:T(8,128)(2,1)} %param.41) | copy-start | bytes 1179652
  375.1 119.9 %all-gather.17.cloned.1.call-start = ((), (), s32[]{:S(2)}) async-start(), calls=%async_computation.10 | async-start | bytes 1966080 | tf_op jit(solution)/shard_map/all_gather | solution.py:95
  463.9 7.6 copy-start.13
  463.9 359.9 %reduce-scatter.11.cloned.1.call-start = ((), (), s32[]{:S(2)}) async-start(), calls=%async_computation.11 | async-start | bytes 3932160 | tf_op jit(solution)/shard_map/reduce_scatter | solution.py:106
  479.9 3.9 copy-start.71
  479.9 3.9 copy-start.77
  484.9 12.2 %copy-start.53 = (f32[1024,1,3,64]{0,3,2,1:T(8,128)S(1)}, f32[1024,1,3,64]{0,3,2,1:T(8,128)}, u32[]{:S(2)}) copy-start(f32[1024,1,3,64]{0,3,2,1:T(8,128)} %reshape.1347) | copy-start | bytes 2359300
  484.9 12.2 %copy-start.78 = (f32[1024,3]{0,1:T(4,128)S(1)}, f32[1024,3]{0,1:T(4,128)}, u32[]{:S(2)}) copy-start(f32[1024,3]{0,1:T(4,128)} %div.228) | copy-start | bytes 36868
  667.3 6.7 copy-start.6
  667.3 6.7 copy-start.19
  678.0 4.2 copy-start.79
  682.2 15.2 %copy-start.62 = (f32[16,64,1,3]{1,3,0,2:T(4,128)S(1)}, f32[16,64,1,3]{1,3,0,2:T(4,128)}, u32[]{:S(2)}) copy-start(f32[16,64,1,3]{1,3,0,2:T(4,128)} %copy-done.59) | copy-start | bytes 36868
  682.2 15.2 %copy-start.93 = (f32[16,64,3]{1,0,2:T(8,128)S(1)}, f32[16,64,3]{1,0,2:T(8,128)}, u32[]{:S(2)}) copy-start(f32[16,64,3]{1,0,2:T(8,128)} %neg.56) | copy-start | bytes 36868
  698.1 20.2 %copy-start.25 = (f32[1,3,128,64]{3,2,1,0:T(8,128)S(1)}, f32[1,3,128,64]{3,2,1,0:T(8,128)}, u32[]{:S(2)}) copy-start(f32[1,3,128,64]{3,2,1,0:T(8,128)} %custom-call.6) | copy-start | bytes 294916
  698.1 20.2 %copy-start.98 = (f32[1,3,128]{2,1,0:T(4,128)S(1)}, f32[1,3,128]{2,1,0:T(4,128)}, u32[]{:S(2)}) copy-start(f32[1,3,128]{2,1,0:T(4,128)} %custom-call.7) | copy-start | bytes 4612
  698.1 20.2 %copy-start.134 = (f32[4]{0:T(128)S(1)}, f32[4]{0:T(128)}, u32[]{:S(2)}) copy-start(f32[4]{0:T(128)} %reverse) | copy-start | bytes 52
  718.3 9.3 copy-start.89
  743.4 4.0 copy-start.35
  749.5 5.9 copy-start.68
  752.6 6.2 copy-start.41
  774.7 199.2 %all-reduce.8.cloned.1.call-start = ((), (), s32[]{:S(2)}) async-start(), calls=%async_computation.12 | async-start | bytes 14155776 | tf_op jit(solution)/shard_map/psum | solution.py:380
  777.6 4.9 copy-start.129
  777.6 4.9 copy-start.133
  777.6 4.9 copy-start.138
  794.7 29.1 %copy-start.22 = (bf16[256,1,768]{2,0,1:T(8,128)(2,1)S(1)}, bf16[256,1,768]{2,0,1:T(8,128)(2,1)}, u32[]{:S(2)}) copy-start(bf16[256,1,768]{2,0,1:T(8,128)(2,1)} %param.25) | copy-start | bytes 1179652
  794.7 29.1 %copy-start.107 = (f32[768]{0:T(1024)S(1)}, f32[768]{0:T(1024)}, u32[]{:S(2)}) copy-start(f32[768]{0:T(1024)} %param.27) | copy-start | bytes 9220
  794.7 29.1 %copy-start.112 = (f32[256]{0:T(256)S(1)}, f32[256]{0:T(256)}, u32[]{:S(2)}) copy-start(f32[256]{0:T(256)} %copy-done.111) | copy-start | bytes 3076
  794.7 29.1 %copy-start.116 = (f32[256]{0:T(256)S(1)}, f32[256]{0:T(256)}, u32[]{:S(2)}) copy-start(f32[256]{0:T(256)} %copy-done.115) | copy-start | bytes 3076
  795.3 30.1 %copy-start.49 = (f32[256,1,768]{2,0,1:T(8,128)S(1)}, f32[256,1,768]{2,0,1:T(8,128)}, u32[]{:S(2)}) copy-start(f32[256,1,768]{2,0,1:T(8,128)} %get-tuple-element.1030) | copy-start | bytes 2359300
  977.6 3.9 copy-start.1
  (85 other events, 199.0 us)
Sparse Core Ops, SparseCore 0:
  12.0 33.7 all-gather.10
  248.5 42.2 reduce-scatter.4
  294.8 30.9 all-gather.12
  327.5 30.9 all-gather.14
  369.4 43.9 reduce-scatter.8
  416.3 43.9 reduce-scatter.6
  464.0 30.9 all-gather.16
  774.8 42.2 reduce-scatter.10
  820.8 152.9 all-reduce.7
where the time goes:
time: 995 us; the launch traced here: 988 us
  waiting for transfers between devices  311 us (31%)
  local copies, waits for them, and re-layouts  225 us (23%)
  blocking collectives  148 us (15%)
  other arithmetic  123 us (12%)
  matrix products  111 us (11%)
  loops' own time  50.9 us (5%)
  between operations  16.8 us (2%)
    psum x1, waiting for transfers between devices, shards(): lax.psum((grad_w_qkv, grad_b_qkv, grad_w_feat, grad_b_feat, output_weight...  107 us
    dynamic_slice x96, local copies, waits for them, and re-layouts, shards(): lax.scan(pass_on, empty_state, (seg_tail.astype(single_float), tail_state...  86.9 us
    reduce_scatter x2, waiting for transfers between devices, reduce_rows(): lax.psum_scatter(term_fn(jnp.int32(0), local_rows * lax.axis_size('tp')),...  85.9 us
    all_gather x4, waiting for transfers between devices, widen_rows(): return lax.all_gather(rounded, 'tp', axis=0, tiled=True)  79.4 us
    all_gather x4, blocking collectives, prefix(): pieces = jax.tree.map(lambda part: lax.all_gather(part, axis), value)  67.5 us
    dynamic_update_slice x64, other arithmetic, shards(): lax.scan(pass_on, empty_state, (seg_tail.astype(single_float), tail_state...  42.1 us
    psum x1, blocking collectives, shards(): lax.psum((jnp.sum(gain_one_rows, axis=(0, 1)), jnp.sum(grad_normed_one, a...  39 us
    reduce_scatter x2, waiting for transfers between devices, reduce_grads(): lax.psum_scatter(term_fn(jnp.int32(0), local_rows * lax.axis_size('tp')),...  38.3 us
  transfers between devices with their start and end apart: 9, of which 8 were waited for; matrix products, arithmetic and copies ran while one was open for 6% of the time, Pallas kernels for 0%

commit v1 on v0

v1 whole, which is shorter than its diff:
```python
import functools
import math

import jax
import jax.numpy as jnp
from jax import lax
from jax.experimental import pallas as pl
from jax.experimental.pallas import tpu as pltpu
from jax.sharding import PartitionSpec as P

f32 = jnp.float32
bf16 = jnp.bfloat16
EPS = 1e-05
ROOT = math.sqrt(2.0 / math.pi)
VMEM_LIMIT = 48 * 1024 * 1024


def nn(a, b):
    return jnp.dot(a, b, preferred_element_type=f32)


def nt(a, b):
    return lax.dot_general(a, b, (((1,), (1,)), ((), ())), preferred_element_type=f32)


def tn(a, b):
    return lax.dot_general(a, b, (((0,), (0,)), ((), ())), preferred_element_type=f32)


def call(kernel, outs, args, smem=0, scratch=(), flops=1, name=None):
    specs = [pl.BlockSpec(memory_space=pltpu.SMEM)] * smem
    specs += [pl.BlockSpec(memory_space=pltpu.VMEM)] * (len(args) - smem)
    out_shape = [jax.ShapeDtypeStruct(shape, kind) for shape, kind in outs]
    moved = sum(math.prod(o.shape) * o.dtype.itemsize for o in out_shape)
    moved += sum(math.prod(a.shape) * a.dtype.itemsize for a in args)
    return pl.pallas_call(
        kernel,
        out_shape=out_shape,
        in_specs=specs,
        out_specs=[pl.BlockSpec(memory_space=pltpu.VMEM)] * len(outs),
        scratch_shapes=list(scratch),
        compiler_params=pltpu.CompilerParams(vmem_limit_bytes=VMEM_LIMIT),
        cost_estimate=pl.CostEstimate(flops=flops, bytes_accessed=moved, transcendentals=0),
        name=name,
    )(*args)


def lanes():
    return lax.broadcasted_iota(jnp.int32, (1, 128), 1)


def half_turn(v):
    return pltpu.roll(v, 64, 1)


def norm_stats(v):
    centred = v - jnp.mean(v, axis=-1, keepdims=True)
    inv = lax.rsqrt(jnp.mean(centred * centred, axis=-1, keepdims=True) + EPS)
    return centred * inv, inv


def ln_one_kernel(tok, gain, bias, out):
    hat, _ = norm_stats(tok[...].astype(f32))
    out[...] = (hat * gain[...] + bias[...]).astype(bf16)


def encode(pay, tops, norms):
    for g in range(6):
        pay[g * 64 : g * 64 + 64, :] = tops[g].astype(bf16)
    row = lax.broadcasted_iota(jnp.int32, (16, 128), 0)
    for s in range(2):
        block = jnp.zeros((16, 128), f32)
        for h in range(3):
            n = norms[3 * s + h]
            high = n.astype(bf16).astype(f32)
            block = jnp.where(row == h, high, block)
            block = jnp.where(row == 3 + h, n - high, block)
        pay[384 + 16 * s : 400 + 16 * s, :] = block.astype(bf16)


def decode(pay, swap=False):
    tops, norms = [], []
    blocks = [pay[384 + 16 * s : 400 + 16 * s, :].astype(f32) for s in range(2)]
    for s in range(2):
        t = 1 - s if swap else s
        for h in range(3):
            g = 3 * t + h
            tops.append(pay[g * 64 : g * 64 + 64, :].astype(f32))
            norms.append(blocks[t][h : h + 1, :] + blocks[t][3 + h : 4 + h, :])
    return tops, norms


PAY = (416, 128)


def combine(parts):
    tops = [sum(f * p[0][g] for f, p in parts) for g in range(6)]
    norms = [sum(f * p[1][g] for f, p in parts) for g in range(6)]
    return tops, norms


def qkv_kernel(
    idx, seg, n_own, n_oth, w_own, w_oth, bias, wfe, bfe, ln_bias, segc,
    ncat, u, fq, fk, va, arow, pay,
):
    x, y = idx[0], idx[1]
    lane = lanes()
    low = lane < 64
    centre = jnp.broadcast_to(ln_bias[...], (16, 768)).astype(bf16)
    for s, w in ((0, w_own), (1, w_oth)):
        a01 = nt(centre, w[384:512, :])[0:1] + bias[s, :, 384:512]
        a12 = nt(centre, w[448:576, :])[0:1] + bias[s, :, 448:576]
        arow[3 * s] = jnp.where(low, a01, 0.0)
        arow[3 * s + 1] = jnp.where(low, a12, 0.0)
        arow[3 * s + 2] = jnp.where(low, half_turn(jnp.broadcast_to(a12, (8, 128)))[0:1], 0.0)
    for r, n_ref in ((0, n_own), (1, n_oth)):
        start = pl.multiple_of((x if r == 0 else 1 - x) * 256, 256)
        rows = pl.ds(start, 256)
        n = n_ref[...]
        ncat[rows, :] = n
        for s, w in ((0, w_own), (1, w_oth)):
            qk = (nt(n, w[0:384, :]) + bias[s, :, 0:384]).astype(bf16)
            u[rows, 384 * s : 384 * s + 384] = qk
            for p in range(3):
                logits = nn(qk[:, 128 * p : 128 * p + 128], wfe[s, p]) + bfe[s, p]
                for k in range(2):
                    part = logits[:, 128 * k : 128 * k + 128]
                    top = jnp.max(part, axis=1, keepdims=True)
                    e = jnp.exp(part - top)
                    soft = (e * (1.0 / jnp.sum(e, axis=1, keepdims=True))).astype(bf16)
                    m = 2 * p + k
                    if m < 3:
                        fq[3 * s + m, rows, :] = soft
                    else:
                        fk[3 * s + m - 3, rows, :] = soft
            v01 = (nt(n, w[384:512, :]) + bias[s, :, 384:512]).astype(bf16).astype(f32)
            v12 = (nt(n, w[448:576, :]) + bias[s, :, 448:576]).astype(bf16).astype(f32)
            ones = jnp.where((lane == 64) | (lane == 65), 1.0, 0.0)
            for h, v in ((0, v01), (1, v12), (2, half_turn(v12))):
                va[3 * s + h, rows, :] = jnp.where(low, v - arow[3 * s + h], ones).astype(bf16)
    last = seg[y * 512 + 511]
    keep = (segc[...] == last).astype(f32)
    tops, norms = [], []
    for g in range(6):
        st = tn(va[g], (fk[g].astype(f32) * keep).astype(bf16))
        tops.append(st[0:64])
        norms.append(st[64:65])
    encode(pay, tops, norms)


def inner_kernel(segc, segr, fq, fk, va, numden):
    for it in range(2):
        wide = 256 * (it + 1)
        i = lax.broadcasted_iota(jnp.int32, (256, wide), 0) + 256 * it
        j = lax.broadcasted_iota(jnp.int32, (256, wide), 1)
        mask = ((j <= i) & (segc[256 * it : 256 * it + 256, :] == segr[:, 0:wide])).astype(f32)

        def body(g, carry):
            scores = nt(fq[g, 256 * it : 256 * it + 256, :], fk[g, 0:wide, :])
            weights = (scores * mask).astype(bf16)
            numden[g, 256 * it : 256 * it + 256, :] = nn(weights, va[g, 0:wide, :])
            return carry

        lax.fori_loop(0, 6, body, 0)


def flag(test):
    return jnp.where(test, 1.0, 0.0).astype(f32)


def send_state_kernel(forward, idx, seg, mine, theirs, out):
    y = idx[1]
    if forward:
        first_half = flag(seg[511] == seg[1023])
        own = jnp.where(y == 0, first_half, 1.0)
        oth = jnp.where(y == 0, 1.0, first_half)
    else:
        second_half = flag(seg[512] == seg[0])
        own = jnp.where(y == 0, 1.0, second_half)
        oth = jnp.where(y == 0, second_half, 1.0)
    tops, norms = combine([(own, decode(mine)), (oth, decode(theirs, True))])
    encode(out, tops, norms)


def carry_state(forward, idx, seg, theirs, one, two, three):
    y = idx[1]
    near = flag(seg[511] == seg[512])
    if forward:
        near = jnp.where(y == 1, near, 0.0)
        far = jnp.where(y == 1, flag(seg[0] == seg[512]), 1.0)
    else:
        near = jnp.where(y == 0, near, 0.0)
        far = jnp.where(y == 0, flag(seg[511] == seg[1023]), 1.0)
    return combine(
        [(near, decode(theirs, True)), (far, decode(one)), (far, decode(two)), (far, decode(three))]
    )


def augmented(top, norm, third):
    row = lax.broadcasted_iota(jnp.int32, (64, 128), 0)
    high = norm.astype(bf16).astype(f32)
    rest = norm - high
    if third:
        low = jnp.where(row < 2, high, jnp.where(row == 2, rest, 0.0))
    else:
        low = jnp.where(row == 0, high, jnp.where(row == 1, rest, 0.0))
    return jnp.concatenate([top, low], axis=0).astype(bf16)


def out_kernel(
    idx, seg, theirs, one, two, three, numden, fq, arow, segc, w_own, w_oth,
    att, mixed, paug, part_own, part_oth,
):
    x, y = idx[0], idx[1]
    tops, norms = carry_state(True, idx, seg, theirs, one, two, three)
    low = lanes() < 64
    first = seg[y * 512]
    open_rows = (segc[...] == first).astype(f32)
    for s in range(2):
        heads = []
        for h in range(3):
            g = 3 * s + h
            paug[g] = augmented(tops[g], norms[g], True)
            nd = numden[g] + open_rows * nt(fq[g], paug[g])
            inv = 1.0 / (nd[:, 64:65] + nd[:, 66:67])
            a = jnp.where(low, nd * inv, 0.0)
            att[g] = jnp.where(low, a, inv)
            heads.append(a + arow[g])
        mixed[:, 256 * s : 256 * s + 128] = (heads[0] + half_turn(heads[1])).astype(bf16)
        mixed[:, 256 * s + 128 : 256 * s + 256] = half_turn(heads[2]).astype(bf16)

    def term(start):
        rows = pl.ds(pl.multiple_of(start * 256, 256), 256)
        total = nn(mixed[rows, 0:128], w_own[0:128, :]) + nn(mixed[rows, 128:256], w_own[64:192, :])
        total += nn(mixed[rows, 256:384], w_oth[0:128, :])
        return total + nn(mixed[rows, 384:512], w_oth[64:192, :])

    part_oth[...] = term(1 - x).astype(bf16)
    part_own[...] = term(x)


def ln_two_kernel(tok, own, recv, b_out, gain, bias, mid, normed):
    v = tok[...].astype(f32) + (own[...] + recv[...].astype(f32) + b_out[...])
    mid[...] = v
    hat, _ = norm_stats(v)
    normed[...] = (hat * gain[...] + bias[...]).astype(bf16)


def mlp_kernel(n2, cot, up_own, up_oth, down_own, down_oth, b_up, hid, gpre, gn2):
    rows = n2[...]
    cots = cot[...]
    total = jnp.zeros((256, 768), f32)
    for s, up, down in ((0, up_own, down_own), (1, up_oth, down_oth)):
        for t in range(3):
            cols = slice(256 * t, 256 * t + 256)
            at = slice(768 * s + 256 * t, 768 * s + 256 * t + 256)
            pre = nn(rows, up[:, cols]) + b_up[s, :, cols]
            grad = nt(cots, down[cols, :])
            square = pre * pre
            th = jnp.tanh(ROOT * (pre + 0.044715 * (square * pre)))
            half = 0.5 * (1.0 + th)
            hid[:, at] = (pre * half).astype(bf16)
            slope = half + 0.5 * pre * (1.0 - th * th) * (ROOT * (1.0 + 3 * 0.044715 * square))
            g = (grad * slope).astype(bf16)
            gpre[:, at] = g
            total += nt(g, up[:, cols])
    gn2[...] = total.astype(gn2.dtype)


def down_kernel(hid_own, hid_oth, down_own, down_oth, own, oth):
    oth[...] = (nn(hid_oth[:, 0:768], down_own[...]) + nn(hid_oth[:, 768:1536], down_oth[...])).astype(bf16)
    own[...] = nn(hid_own[:, 0:768], down_own[...]) + nn(hid_own[:, 768:1536], down_oth[...])


def final_kernel(mid, own, recv, b_down, out):
    out[...] = (mid[...] + (own[...] + recv[...].astype(f32)) + b_down[...]).astype(bf16)


def norm_grad(v, gain, grad):
    hat, inv = norm_stats(v)
    e = grad * gain
    back = inv * (e - jnp.mean(e, axis=-1, keepdims=True) - hat * jnp.mean(e * hat, axis=-1, keepdims=True))
    return back, jnp.sum(grad * hat, axis=0, keepdims=True), jnp.sum(grad, axis=0, keepdims=True)


def put_vector(ref, row, vec):
    for t in range(vec.shape[1] // 128):
        ref[row + t : row + t + 1, :] = vec[:, 128 * t : 128 * t + 128]


def ln_two_back_kernel(mid, own, recv, gain, cot, gmid, branch, vecs):
    cots = cot[...].astype(f32)
    back, dgain, dbias = norm_grad(mid[...], gain[...], own[...] + recv[...].astype(f32))
    g = cots + back
    gmid[...] = g
    low = g.astype(bf16)
    branch[...] = low
    put_vector(vecs, 0, jnp.sum(low.astype(f32), axis=0, keepdims=True))
    put_vector(vecs, 6, dgain)
    put_vector(vecs, 12, dbias)
    put_vector(vecs, 18, jnp.sum(cots, axis=0, keepdims=True))


def ln_one_back_kernel(tok, own, recv, gain, gmid, out, vecs):
    back, dgain, dbias = norm_grad(tok[...].astype(f32), gain[...], own[...] + recv[...].astype(f32))
    out[...] = gmid[...] + back
    put_vector(vecs, 0, dgain)
    put_vector(vecs, 6, dbias)


def mlp_send_kernel(idx, hid_own, hid_oth, gpre_own, gpre_oth, n2_own, n2_oth, cot_own, cot_oth, send):
    at = pl.ds(pl.multiple_of((1 - idx[3]) * 384, 384), 384)
    for s in range(2):
        units = pl.ds(pl.multiple_of((1 - idx[3]) * 384 + 768 * s, 384), 384)
        cols = slice(768 * s, 768 * s + 768)
        send[s, 0:384, :] = (tn(hid_own[:, units], cot_own[...]) + tn(hid_oth[:, units], cot_oth[...])).astype(bf16)
        send[s, 384:768, :] = (tn(n2_own[:, at], gpre_own[:, cols]) + tn(n2_oth[:, at], gpre_oth[:, cols])).astype(bf16)


def mlp_keep_kernel(idx, hid_own, hid_oth, gpre_own, gpre_oth, n2_own, n2_oth, cot_own, cot_oth, recv, keep, send, sums):
    at = pl.ds(pl.multiple_of(idx[3] * 384, 384), 384)
    for s in (1, 0):
        units = pl.ds(pl.multiple_of(idx[3] * 384 + 768 * s, 384), 384)
        cols = slice(768 * s, 768 * s + 768)
        down = tn(hid_own[:, units], cot_own[...]) + tn(hid_oth[:, units], cot_oth[...])
        down += recv[s, 0:384, :].astype(f32)
        up = tn(n2_own[:, at], gpre_own[:, cols]) + tn(n2_oth[:, at], gpre_oth[:, cols])
        up += recv[s, 384:768, :].astype(f32)
        if s == 1:
            send[0:384, :] = down.astype(bf16)
            send[384:768, :] = up.astype(bf16)
        else:
            keep[0:384, :] = down
            keep[384:768, :] = up
        bias = jnp.sum(gpre_own[:, cols].astype(f32), axis=0, keepdims=True)
        bias += jnp.sum(gpre_oth[:, cols].astype(f32), axis=0, keepdims=True)
        sums[s] = jnp.zeros((8, 128), f32)
        for t in range(6):
            sums[s, t : t + 1, :] = bias[:, 128 * t : 128 * t + 128]


def grad_mixed_kernel(idx, seg, gb_own, gb_oth, w_own, w_oth, att, fq, segc, gbcat, gna, pay):
    x, y = idx[0], idx[1]
    lane = lanes()
    low = lane < 64
    gbcat[pl.ds(pl.multiple_of(x * 256, 256), 256), :] = gb_own[...]
    gbcat[pl.ds(pl.multiple_of((1 - x) * 256, 256), 256), :] = gb_oth[...]
    first = seg[y * 512]
    open_rows = (segc[...] == first).astype(f32)
    tops, norms = [], []
    for s, w in ((0, w_own), (1, w_oth)):
        g01 = nt(gbcat[...], w[0:128, :]).astype(bf16).astype(f32)
        g12 = nt(gbcat[...], w[64:192, :]).astype(bf16).astype(f32)
        for h, gm in ((0, g01), (1, g12), (2, half_turn(g12))):
            g = 3 * s + h
            a = att[g]
            gn = jnp.where(low, gm * a[:, 64:65], 0.0).astype(bf16).astype(f32)
            gd = -jnp.sum(gn * a, axis=1, keepdims=True)
            high = gd.astype(bf16).astype(f32)
            tail = jnp.where((lane == 64) | (lane == 66), high, jnp.where(lane == 65, gd - high, 0.0))
            gna[g] = jnp.where(low, gn, tail).astype(bf16)
            st = tn(gna[g], (fq[g].astype(f32) * open_rows).astype(bf16))
            tops.append(st[0:64])
            norms.append(st[64:65] + st[65:66])
    encode(pay, tops, norms)


def soft_grad(soft, grad):
    s = soft.astype(f32)
    return (s * (grad - jnp.sum(grad * s, axis=1, keepdims=True))).astype(bf16)


def inner_back_kernel(idx, seg, segc, segr, fq, fk, va, gna, paug, gq, gkf, gv):
    y = idx[1]
    first = seg[y * 512]
    i0 = lax.broadcasted_iota(jnp.int32, (256, 256), 0)
    j0 = lax.broadcasted_iota(jnp.int32, (256, 256), 1)
    for it in range(2):
        rows = slice(256 * it, 256 * it + 256)
        wide = 256 * (it + 1)
        i = lax.broadcasted_iota(jnp.int32, (256, wide), 0) + 256 * it
        j = lax.broadcasted_iota(jnp.int32, (256, wide), 1)
        mask = ((j <= i) & (segc[rows, :] == segr[:, 0:wide])).astype(f32)
        open_rows = (segc[rows, :] == first).astype(f32)

        def queries(g, carry):
            gw = (nt(gna[g, rows, :], va[g, 0:wide, :]) * mask).astype(bf16)
            grad = nn(gw, fk[g, 0:wide, :]) + open_rows * nn(gna[g, rows, :], paug[g])
            gq[g, rows, :] = soft_grad(fq[g, rows, :], grad)
            return carry

        lax.fori_loop(0, 6, queries, 0)
        tall = 512 - 256 * it
        kj = lax.broadcasted_iota(jnp.int32, (256, tall), 0)
        ki = lax.broadcasted_iota(jnp.int32, (256, tall), 1)
        kmask = ((kj <= ki) & (segc[rows, :] == segr[:, 256 * it : 512])).astype(f32)

        def keys(g, carry):
            late = slice(256 * it, 512)
            w = (nt(fk[g, rows, :], fq[g, late, :]) * kmask).astype(bf16)
            gv[g, rows, :] = nn(w, gna[g, late, :])
            gw = (nt(va[g, rows, :], gna[g, late, :]) * kmask).astype(bf16)
            gkf[g, rows, :] = nn(gw, fq[g, late, :])
            return carry

        lax.fori_loop(0, 6, keys, 0)


def qkv_back_kernel(
    idx, seg, theirs, one, two, three, segc, fk, va, gkf, gv, gq, wfe, w_own, w_oth,
    gk, gproj, part_own, part_oth,
):
    x, y = idx[0], idx[1]
    tops, norms = carry_state(False, idx, seg, theirs, one, two, three)
    low = lanes() < 64
    last = seg[y * 512 + 511]
    open_rows = (segc[...] == last).astype(f32)
    for s in range(2):
        base = 640 * s
        values = []
        for h in range(3):
            g = 3 * s + h
            aug = augmented(tops[g], norms[g], False)
            grad = gkf[g] + open_rows * nn(va[g], aug)
            gk[g] = soft_grad(fk[g], grad)
            values.append(jnp.where(low, gv[g] + open_rows * nt(fk[g], aug), 0.0))
        gproj[:, base + 384 : base + 512] = (values[0] + half_turn(values[1])).astype(bf16)
        gproj[:, base + 512 : base + 640] = half_turn(values[2]).astype(bf16)
        order = [gq[3 * s], gq[3 * s + 1], gq[3 * s + 2], gk[3 * s], gk[3 * s + 1], gk[3 * s + 2]]
        for p in range(3):
            pair = jnp.concatenate([order[2 * p], order[2 * p + 1]], axis=1)
            gproj[:, base + 128 * p : base + 128 * p + 128] = nt(pair, wfe[s, p]).astype(bf16)

    def term(start):
        rows = pl.ds(pl.multiple_of(start * 256, 256), 256)
        total = nn(gproj[rows, 0:512], w_own[0:512, :]) + nn(gproj[rows, 512:640], w_own[448:576, :])
        total += nn(gproj[rows, 640:1152], w_oth[0:512, :])
        return total + nn(gproj[rows, 1152:1280], w_oth[448:576, :])

    part_oth[...] = term(1 - x).astype(bf16)
    part_own[...] = term(x)


def attn_weights_kernel(idx, n, gproj, mixed, gb, u, gq, gk, send, keep, sums, scr):
    c = idx[3]
    row = lax.broadcasted_iota(jnp.int32, (8, 128), 0)
    for s in range(2):
        base = 640 * s
        scr[0:512, :] = tn(gproj[:, base : base + 512], n[...])
        scr[512:576, :] = tn(gproj[:, base + 512 : base + 640], n[...])[64:128]
        scr[576:704, :] = tn(mixed[:, 256 * s : 256 * s + 128], gb[...])
        scr[704:768, :] = tn(mixed[:, 256 * s + 128 : 256 * s + 256], gb[...])[64:128]
        mine, other = pl.multiple_of(288 * c, 32), pl.multiple_of(288 * (1 - c), 32)
        mine_out, other_out = pl.multiple_of(576 + 96 * c, 32), pl.multiple_of(576 + 96 * (1 - c), 32)
        keep[s, 0:288, :] = scr[pl.ds(mine, 288), :]
        keep[s, 288:384, :] = scr[pl.ds(mine_out, 96), :]
        send[s, 0:288, :] = scr[pl.ds(other, 288), :].astype(bf16)
        send[s, 288:384, :] = scr[pl.ds(other_out, 96), :].astype(bf16)
        order = [gq[3 * s], gq[3 * s + 1], gq[3 * s + 2], gk[3 * s], gk[3 * s + 1], gk[3 * s + 2]]
        feats = [jnp.zeros((64, 128), f32)] * 3
        biases = [jnp.zeros((1, 128), f32)] * 3
        for p in range(3):
            pair = jnp.concatenate([order[2 * p], order[2 * p + 1]], axis=1)
            prod = tn(u[:, 384 * s + 128 * p : 384 * s + 128 * p + 128], pair)
            for k in range(2):
                block = prod[64 * k : 64 * k + 64, 128 * k : 128 * k + 128]
                h = (2 * p + k) % 3
                feats[h] = feats[h] + (block - half_turn(block))
                total = jnp.sum(order[2 * p + k].astype(f32), axis=0, keepdims=True)
                total8 = jnp.broadcast_to(total, (8, 128))
                biases[h] = biases[h] + (total8 - half_turn(total8))[0:1]
        for h in range(3):
            sums[s, 64 * h : 64 * h + 64, :] = feats[h]
        block = jnp.zeros((8, 128), f32)
        for t in range(5):
            total = jnp.sum(gproj[:, base + 128 * t : base + 128 * t + 128].astype(f32), axis=0, keepdims=True)
            block = jnp.where(row == t, total, block)
        for h in range(3):
            block = jnp.where(row == 5 + h, biases[h], block)
        sums[s, 192:200, :] = block


def after(value, *deps):
    return lax.optimization_barrier((value,) + deps)[0]


def swap(value, axis, bit):
    count = lax.axis_size(axis)
    return jax.tree.map(
        lambda v: lax.ppermute(v, axis, [(i, i ^ bit) for i in range(count)]), value
    )


def shift(value, axis, step):
    count = lax.axis_size(axis)
    pairs = [(i, i + step) for i in range(count) if 0 <= i + step < count]
    return lax.ppermute(value, axis, pairs)


def other_shard(half, c):
    fetched = swap(half, "tp", 2)
    sibling = swap(fetched, "dp", 1)
    return jnp.concatenate(
        [jnp.where(c == 0, fetched, sibling), jnp.where(c == 0, sibling, fetched)], axis=0
    )


def my_half(value, c):
    rows = value.shape[0] // 2
    return jnp.where(c == 0, value[:rows], value[rows:])


def rest_of_dp(value):
    bit = 2
    while bit < lax.axis_size("dp"):
        value = jax.tree.map(lambda v: v + swap(v.astype(bf16), "dp", bit).astype(f32), value)
        bit *= 2
    return value


def over_cp(keep, z):
    rows = keep.shape[0] // 2
    low = (z & 1) == 0
    mine = jnp.where(low, keep[:rows], keep[rows:])
    sent = jnp.where(low, keep[rows:], keep[:rows]).astype(bf16)
    half = (mine + swap(sent, "cp", 1).astype(f32)).astype(bf16)
    bit = 2
    while bit < lax.axis_size("cp"):
        half = (half.astype(f32) + swap(half, "cp", bit).astype(f32)).astype(bf16)
        bit *= 2
    return half, swap(half, "cp", 1)


def whole_rows(pieces, c, z):
    half, pair = pieces
    low = (z & 1) == 0
    mine = jnp.concatenate([jnp.where(low, half, pair), jnp.where(low, pair, half)], axis=0)
    sibling = swap(mine, "dp", 1)
    return jnp.where(c == 0, mine, sibling).astype(f32), jnp.where(c == 0, sibling, mine).astype(f32)


def shards(
    tokens, segment_ids, ln1_gain, ln1_bias, w_qkv, b_qkv, w_feat, b_feat, output_weight, b_out,
    ln2_gain, ln2_bias, w_up, b_up, w_down, b_down, cotangent,
):
    t = lax.axis_index("tp")
    z = lax.axis_index("cp")
    c = lax.axis_index("dp") & 1
    x, y = t & 1, t >> 1
    idx = jnp.stack([x, y, z, c, c, c, c, c]).astype(jnp.int32)
    row = lambda v: v.reshape(1, -1)
    tok = tokens.reshape(256, 768)
    cot_own = cotangent.reshape(256, 768)
    seg = segment_ids.reshape(1024)
    seg_block = lax.dynamic_slice_in_dim(seg, y * 512, 512, 0)
    segc = seg_block.reshape(512, 1)
    segr = seg_block.reshape(1, 512)

    wq_own = jnp.transpose(w_qkv, (1, 2, 0)).reshape(576, 768)
    wq_oth = other_shard(my_half(wq_own, c), c)
    flat = jnp.concatenate([b_qkv.reshape(-1), b_feat.reshape(-1), b_up])
    flat_oth = swap(flat, "tp", 2)
    feat_oth = swap(w_feat, "tp", 2)
    biases = jnp.stack([flat, flat_oth])[:, None, :]
    bq = biases[:, :, 0:576]
    bf = biases[:, :, 576:768].reshape(2, 3, 64)
    bup = biases[:, :, 768:1536]
    wf = jnp.stack([w_feat, feat_oth])
    signed = jnp.concatenate([wf, -wf], axis=-1)
    pick_a, pick_b = (0, 2, 1), (1, 0, 2)
    take = lambda v, picks: jnp.stack([v[:, i] for i in picks], axis=1)
    wfe = jnp.pad(take(signed, pick_a), ((0, 0), (0, 0), (0, 64), (0, 128))) + jnp.pad(
        take(signed, pick_b), ((0, 0), (0, 0), (64, 0), (128, 0))
    )
    bsigned = jnp.concatenate([bf, -bf], axis=-1)
    bfe = jnp.concatenate([take(bsigned, pick_a), take(bsigned, pick_b)], axis=-1)[:, :, None, :]

    (n_own,) = call(ln_one_kernel, [((256, 768), bf16)], [tok, row(ln1_gain), row(ln1_bias)], name="ln_one")
    n_oth = swap(n_own, "tp", 1)
    cot_oth = swap(after(cot_own, n_oth), "tp", 1)
    out_half = after(my_half(output_weight, c), wq_oth)
    wo_oth = other_shard(out_half, c)
    up_oth = other_shard(after(my_half(w_up, c), wo_oth), c)
    down_oth = other_shard(after(my_half(w_down, c), up_oth), c)

    head_rows = ((6, 512, 128), bf16)
    head_rows_f32 = ((6, 512, 128), f32)
    ncat, u, fq, fk, va, arow, pay = call(
        qkv_kernel,
        [((512, 768), bf16), ((512, 768), bf16), head_rows, head_rows, head_rows, ((6, 1, 128), f32), (PAY, bf16)],
        [idx, seg, n_own, n_oth, wq_own, wq_oth, bq, wfe, bfe, row(ln1_bias), segc],
        smem=2, flops=2 * 10**9, name="qkv",
    )
    pay_y = swap(pay, "tp", 2)
    (numden,) = call(inner_kernel, [head_rows_f32], [segc, segr, fq, fk, va], flops=10**9, name="inner")
    (state,) = call(
        functools.partial(send_state_kernel, True), [(PAY, bf16)], [idx, seg, pay, pay_y], smem=2, name="state"
    )
    carried = [shift(state, "cp", k) for k in (1, 2, 3)]
    att, mixed, paug, part_own, part_oth = call(
        out_kernel,
        [head_rows_f32, ((512, 512), bf16), ((6, 128, 128), bf16), ((256, 768), f32), ((256, 768), bf16)],
        [idx, seg, pay_y, *carried, numden, fq, arow, segc, output_weight, wo_oth],
        smem=2, flops=10**9, name="out",
    )
    part_in = swap(part_oth, "tp", 1)

    mid, n2_own = call(
        ln_two_kernel, [((256, 768), f32), ((256, 768), bf16)],
        [tok, part_own, part_in, row(b_out), row(ln2_gain), row(ln2_bias)], name="ln_two",
    )
    n2_oth = swap(n2_own, "tp", 1)

    def mlp(n2, cot, kind):
        return call(
            mlp_kernel, [((256, 1536), bf16), ((256, 1536), bf16), ((256, 768), kind)],
            [n2, cot, w_up, up_oth, w_down, down_oth, bup], flops=2 * 10**9, name="mlp",
        )

    hid_own, gpre_own, gn2_own = mlp(n2_own, cot_own, f32)
    hid_oth, gpre_oth, gn2_oth = mlp(n2_oth, cot_oth, bf16)
    gn2_in = swap(gn2_oth, "tp", 1)
    gmid, gb_own, vecs_two = call(
        ln_two_back_kernel, [((256, 768), f32), ((256, 768), bf16), ((24, 128), f32)],
        [mid, gn2_own, gn2_in, row(ln2_gain), cot_own], name="ln_two_back",
    )
    gb_oth = swap(gb_own, "tp", 1)

    mlp_args = [idx, hid_own, hid_oth, gpre_own, gpre_oth, n2_own, n2_oth, cot_own, cot_oth]
    (mlp_send,) = call(mlp_send_kernel, [((2, 768, 768), bf16)], mlp_args, smem=1, flops=2 * 10**9, name="mlp_send")
    mlp_recv = swap(mlp_send, "dp", 1)
    mlp_keep, mlp_y, sums_up = call(
        mlp_keep_kernel, [((768, 768), f32), ((768, 768), bf16), ((2, 8, 128), f32)],
        mlp_args + [mlp_recv], smem=1, flops=2 * 10**9, name="mlp_keep",
    )
    mlp_sum = rest_of_dp(mlp_keep + swap(mlp_y, "tp", 2).astype(f32))
    mlp_pieces = [over_cp(mlp_sum[:384], z), over_cp(mlp_sum[384:], z)]
    down_own, down_part = call(
        down_kernel, [((256, 768), f32), ((256, 768), bf16)],
        [hid_own, hid_oth, w_down, down_oth], flops=10**9, name="down",
    )
    down_in = swap(after(down_part, gb_oth), "tp", 1)
    (out_tokens,) = call(final_kernel, [((256, 768), bf16)], [mid, down_own, down_in, row(b_down)], name="final")

    gbcat, gna, gpay = call(
        grad_mixed_kernel, [((512, 768), bf16), head_rows, (PAY, bf16)],
        [idx, seg, gb_own, gb_oth, output_weight, wo_oth, att, fq, segc], smem=2, flops=10**9, name="grad_mixed",
    )
    gpay_y = swap(gpay, "tp", 2)
    (gstate,) = call(
        functools.partial(send_state_kernel, False), [(PAY, bf16)], [idx, seg, gpay, gpay_y], smem=2, name="gstate"
    )
    coming = [shift(gstate, "cp", -k) for k in (1, 2, 3)]
    gq, gkf, gv = call(
        inner_back_kernel, [head_rows, head_rows_f32, head_rows_f32],
        [idx, seg, segc, segr, fq, fk, va, gna, paug], smem=2, flops=3 * 10**9, name="inner_back",
    )
    gk, gproj, gn1_own, gn1_oth = call(
        qkv_back_kernel, [head_rows, ((512, 1280), bf16), ((256, 768), f32), ((256, 768), bf16)],
        [idx, seg, gpay_y, *coming, segc, fk, va, gkf, gv, gq, wfe, wq_own, wq_oth],
        smem=2, flops=2 * 10**9, name="qkv_back",
    )
    gn1_in = swap(gn1_oth, "tp", 1)
    att_send, att_keep, sums_att = call(
        attn_weights_kernel, [((2, 384, 768), bf16), ((2, 384, 768), f32), ((2, 200, 128), f32)],
        [idx, ncat, gproj, mixed, gbcat, u, gq, gk], smem=1,
        scratch=[pltpu.VMEM((768, 768), f32)], flops=2 * 10**9, name="attn_weights",
    )
    att_both = att_keep + swap(att_send, "dp", 1).astype(f32)
    att_sum = rest_of_dp(att_both[0] + swap(att_both[1].astype(bf16), "tp", 2).astype(f32))
    att_pieces = over_cp(att_sum, z)
    d_tok, vecs_one = call(
        ln_one_back_kernel, [((256, 768), f32), ((12, 128), f32)],
        [tok, gn1_own, gn1_in, row(ln1_gain), gmid], name="ln_one_back",
    )

    own_small = jnp.concatenate([sums_att[0], sums_up[0]], axis=0)
    oth_small = jnp.concatenate([sums_att[1], sums_up[1]], axis=0)
    vecs = jnp.concatenate([vecs_two, vecs_one], axis=0)
    count = own_small.shape[0]
    small = jnp.concatenate([own_small, oth_small, vecs], axis=0)
    bit = 1
    while bit < lax.axis_size("dp"):
        small = small + swap(small, "dp", bit)
        bit *= 2
    crossed = swap(small[count:], "tp", 2)
    small = jnp.concatenate([small[:count] + crossed[:count], small[2 * count :] + crossed[count:]], axis=0)
    bit = 1
    while bit < lax.axis_size("cp"):
        small = small + swap(small, "cp", bit)
        bit *= 2
    vec_rows = small[count:] + swap(small[count:], "tp", 1)
    vec = vec_rows.reshape(6, 768)
    d_feat = small[0:192].reshape(3, 64, 128)[:, :, :64]
    tiles = small[192:197].reshape(640)
    d_b_qkv = jnp.concatenate([tiles[:512], tiles[576:640]]).reshape(3, 192)
    d_b_feat = small[197:200, :64]
    d_b_up = small[200:206].reshape(768)

    first, second = whole_rows(mlp_pieces[0], c, z)
    d_w_down = jnp.concatenate([first, second], axis=0)
    first, second = whole_rows(mlp_pieces[1], c, z)
    d_w_up = jnp.concatenate([first, second], axis=0)
    first, second = whole_rows(att_pieces, c, z)
    d_wq = jnp.concatenate([first[:288], second[:288]], axis=0)
    d_w_qkv = jnp.transpose(d_wq.reshape(3, 192, 768), (2, 0, 1))
    d_w_out = jnp.concatenate([first[288:], second[288:]], axis=0)
    return (
        out_tokens.reshape(tokens.shape),
        d_tok.reshape(tokens.shape),
        vec[4],
        vec[5],
        d_w_qkv,
        d_b_qkv,
        d_feat,
        d_b_feat,
        d_w_out,
        vec[0],
        vec[1],
        vec[2],
        d_w_up,
        d_b_up,
        d_w_down,
        vec[3],
    )


def solution(mesh):
    rows = P(("cp", "tp"), "dp", None)
    placed = (
        rows, P("cp", "dp"), P(), P(), P(None, None, "tp"), P(None, "tp"), P("tp", None, None),
        P("tp", None), P("tp", None), P(), P(), P(), P(None, "tp"), P("tp"), P("tp", None), P(), rows,
    )
    given = (
        rows, rows, P(), P(), P(None, None, "tp"), P(None, "tp"), P("tp", None, None), P("tp", None),
        P("tp", None), P(), P(), P(), P(None, "tp"), P("tp"), P("tp", None), P(),
    )
    return jax.shard_map(shards, mesh=mesh, in_specs=placed, out_specs=given, check_vma=False)
```

time: 995 us -> 317 us (0.32)
  local copies, waits for them, and re-layouts: 225 us -> 17.1 us
  waiting for transfers between devices: 311 us -> 157 us
  blocking collectives: 148 us -> 0 us
  matrix products: 111 us -> 0 us
  other arithmetic: 123 us -> 18.7 us
  Pallas kernels: 0 us -> 65.4 us
  starting transfers between devices: 0.54 us -> 56.4 us
  loops' own time: 50.9 us -> 0 us
  between operations: 16.8 us -> 1.67 us
    ppermute x0 -> x47, waiting for transfers between devices: none -> 157 us  [the longest x41 157 us: swap(): lax.ppermute(v, axis, [(i, i ^ bit) for i in range(count)])]
    reduce_scatter x4 -> x0, waiting for transfers between devices: 124 us -> none  [the longest x2 85.9 us: reduce_rows(): lax.psum_scatter(term_fn(jnp.int32(0), local_rows * lax.axis_size('tp')),...]
    psum x1 -> x0, waiting for transfers between devices: 107 us -> none  [shards(): lax.psum((grad_w_qkv, grad_b_qkv, grad_w_feat, grad_b_feat, output_weight...]
    dot_general x37 -> x0, matrix products: 105 us -> none  [the longest x1 6.73 us: shards(): jnp.einsum('nqbhd,nbhfd->nqbhf', gnum_groups, state_in, precision=FULL_PR...]
    dynamic_slice x108 -> x1, local copies, waits for them, and re-layouts: 93.6 us -> 0.01 us  [shards(): seg_block = lax.dynamic_slice_in_dim(seg, y * 512, 512, 0)]
    all_gather x4 -> x0, waiting for transfers between devices: 79.4 us -> none  [widen_rows(): return lax.all_gather(rounded, 'tp', axis=0, tiled=True)]
    all_gather x4 -> x0, blocking collectives: 67.5 us -> none  [prefix(): pieces = jax.tree.map(lambda part: lax.all_gather(part, axis), value)]
    psum x2 -> x0, blocking collectives: 66.9 us -> none  [the longest x1 39 us: shards(): lax.psum((jnp.sum(gain_one_rows, axis=(0, 1)), jnp.sum(grad_normed_one, a...]
  transfers between devices with their start and end apart: 9 -> 47, of which waited for: 8 -> 26; matrix products, arithmetic and copies ran while one was open for 6% -> 7% of each run, Pallas kernels for 0% -> 18%
where the time goes in v1:
time: 317 us; the launch traced here: 316 us
  waiting for transfers between devices  157 us (50%)
  Pallas kernels  65.4 us (21%)
  starting transfers between devices  56.4 us (18%)
  other arithmetic  18.7 us (6%)
  local copies, waits for them, and re-layouts  17.1 us (5%)
    ppermute x41, waiting for transfers between devices, swap(): lax.ppermute(v, axis, [(i, i ^ bit) for i in range(count)])  157 us
    pallas_call x19, Pallas kernels, call(): pl.pallas_call(kernel, out_shape=out_shape, in_specs=specs, out_specs=[pl...  65.4 us
    ppermute x41, starting transfers between devices, swap(): lax.ppermute(v, axis, [(i, i ^ bit) for i in range(count)])  43 us
    ppermute x6, starting transfers between devices, shift(): return lax.ppermute(value, axis, pairs)  13.4 us
    unnamed x113, local copies, waits for them, and re-layouts  10.3 us
  transfers between devices with their start and end apart: 47, of which 26 were waited for; matrix products, arithmetic and copies ran while one was open for 7% of the time, Pallas kernels for 18%

profile of v1, /device:TPU:0, one launch (start us, length us, event | category | flops | bytes accessed | tf_op | source)
XLA Modules:
  0.0 316.3 jit_solution(1391014569827085356)
XLA Ops:
  1.9 3.0 collective-permute-start.1
  4.9 10.2 %collective-permute-done.1 = bf16[288,768]{1,0:T(8,128)(2,1)S(1)} collective-permute-done((bf16[288,768]{1,0:T(8,128)(2,1)S(1)}, bf16[288,768]{1,0:T(8,128)(2,1)S(1)}, u32[]{:S(2)}, u32[]{:S(2)}) %collective-permute-start.1) | collective-permute-done | bytes 442400 | tf_op jit(solution)/shard_map/ppermute | solution.py:490
  15.1 1.8 collective-permute-done.2
  18.0 1.7 collective-permute-start.9
  19.7 4.1 %collective-permute-done.9 = bf16[96,768]{1,0:T(8,128)(2,1)S(1)} collective-permute-done((bf16[96,768]{1,0:T(8,128)(2,1)S(1)}, bf16[96,768]{1,0:T(8,128)(2,1)S(1)}, u32[]{:S(2)}, u32[]{:S(2)}) %collective-permute-start.9) | collective-permute-done | bytes 147488 | tf_op jit(solution)/shard_map/ppermute | solution.py:490
  25.3 1.8 collective-permute-start.12
  27.7 1.7 collective-permute-start.4
  29.7 1.6 collective-permute-start
  31.5 10.3 %collective-permute-done.3 = f32[1536]{0:T(1024)S(1)} collective-permute-done((f32[1536]{0:T(1024)S(1)}, f32[1536]{0:T(1024)S(1)}, u32[]{:S(2)}, u32[]{:S(2)}) %collective-permute-start.3) | collective-permute-done | bytes 6176 | tf_op jit(solution)/shard_map/ppermute | solution.py:490
  42.5 1.8 collective-permute-done.13
  44.3 1.3 broadcast_select_fusion.7
  46.7 1.7 collective-permute-start.14
  48.5 4.7 %qkv.1 = (bf16[512,768]{1,0:T(8,128)(2,1)S(1)}, bf16[512,768]{1,0:T(8,128)(2,1)S(1)}, bf16[6,512,128]{2,1,0:T(8,128)(2,1)S(1)}, bf16[6,512,128]{2,1,0:T(8,128)(2...) custom-call(s32[8]{0:T(128)S(1)} %stack.53.idx, ...), custom_call_target="tpu_custom_call" | custom-call | flops 2000000000 | bytes 7010848 | tf_op jit(solution)/shard_map/qkv/pallas_call | solution.py:36
  55.4 8.9 %collective-permute-done.5.theirs = bf16[416,128]{1,0:T(8,128)(2,1)S(1)} collective-permute-done((bf16[416,128]{1,0:T(8,128)(2,1)S(1)}, bf16[416,128]{1,0:T(8,128)(2,1)S(1)}, u32[]{:S(2)}, u32[]{:S(2)}) %collective-permute-start.5) | collective-permute-done | bytes 106528 | tf_op jit(solution)/shard_map/ppermute | solution.py:490
  65.0 5.7 %collective-permute-start.8 = (bf16[416,128]{1,0:T(8,128)(2,1)S(1)}, bf16[416,128]{1,0:T(8,128)(2,1)S(1)}, u32[]{:S(2)}, u32[]{:S(2)}) collective-permute-start(bf16[416,128]{1,0:T(8,128)(2,1)S(1)} %state.1), channel_id=1, source_target_pairs={{0,6},{1,7},{8,14},{9,15},{16,22},{17,23},{24,30},{25,31}} | collective-permute-start | bytes 319496 | tf_op jit(solution)/shard_map/ppermute | solution.py:497
  70.7 1.3 collective-permute-start.7
  72.0 2.5 collective-permute-start.6
  74.6 4.6 %inner.1.numden = f32[6,512,128]{2,1,0:T(8,128)S(1)} custom-call(s32[512,1]{1,0:T(8,128)S(1)} %copy.41.segc, s32[1,512]{1,0:T(1,128)S(1)} %fusion.23.segr, bf16[6,512,128]{2,1,0:T(8,128)(2,1)S(1)} %get-tuple-element.65.fq, bf16[6,512,128]{2,1,0:T(8,128)(2,1)S(1)} %get-tuple-element.66.fk, bf16[6,512,128]{2,1,0:T(8,128)(2,1)S(1)} %get-tuple-element.67.va), custom_call_target="tpu_custom_call" | custom-call | flops 1000000000 | bytes 3936256 | tf_op jit(solution)/shard_map/inner/pallas_call | solution.py:36
  80.4 3.9 %out.1 = (f32[6,512,128]{2,1,0:T(8,128)S(1)}, bf16[512,512]{1,0:T(8,128)(2,1)S(1)}, bf16[6,128,128]{2,1,0:T(8,128)(2,1)S(1)}, f32[256,768]{1,0:T(8,128)S(1)}, bf16[256,768]{1,0:T(8,128)(2,1)S(1)}) custom-call(s32[8]{0:T(128)S(1)} %stack.53.idx, s32[1024]{0:T(1024)S(1)} %bitcast.67, bf16[416,128]{1,0:T(8,128)(2,1)S(1)} %collective-permute-done.5.theirs, ...), custom_call_target="tpu_custom_call" | custom-call | flops 1000000000 | bytes 6857760 | tf_op jit(solution)/shard_map/out/pallas_call | solution.py:36
  85.1 1.5 collective-permute-start.11
  87.3 9.8 %collective-permute-done.11.recv = bf16[256,768]{1,0:T(8,128)(2,1)S(1)} collective-permute-done((bf16[256,768]{1,0:T(8,128)(2,1)S(1)}, bf16[256,768]{1,0:T(8,128)(2,1)S(1)}, u32[]{:S(2)}, u32[]{:S(2)}) %collective-permute-start.11) | collective-permute-done | bytes 393248 | tf_op jit(solution)/shard_map/ppermute | solution.py:490
  97.4 1.6 collective-permute-start.16
  100.2 4.7 %mlp.2 = (bf16[256,1536]{1,0:T(8,128)(2,1)S(1)}, bf16[256,1536]{1,0:T(8,128)(2,1)S(1)}, f32[256,768]{1,0:T(8,128)S(1)}) custom-call(bf16[256,768]{1,0:T(8,128)(2,1)S(1)} %get-tuple-element.73.n2.n2_own, bf16[256,768]{1,0:T(8,128)(2,1)S(1)} %bitcast.61, bf16[768,768]{1,0:T(8,128)(2,1)S(1)} %copy-done.7, bf16[768,768]{1,0:T(8,128)(2,1)S(1)} %pad_maximum_fusion.1.up_oth, ...), custom_call_target="tpu_custom_call" | custom-call | flops 2000000000 | bytes 7870464 | tf_op jit(solution)/shard_map/mlp/pallas_call | solution.py:36
  105.5 8.0 %collective-permute-done.16.n2.n2_oth = bf16[256,768]{1,0:T(8,128)(2,1)S(1)} collective-permute-done((bf16[256,768]{1,0:T(8,128)(2,1)S(1)}, bf16[256,768]{1,0:T(8,128)(2,1)S(1)}, u32[]{:S(2)}, u32[]{:S(2)}) %collective-permute-start.16) | collective-permute-done | bytes 393248 | tf_op jit(solution)/shard_map/ppermute | solution.py:490
  113.5 4.9 %mlp.3 = (bf16[256,1536]{1,0:T(8,128)(2,1)S(1)}, bf16[256,1536]{1,0:T(8,128)(2,1)S(1)}, bf16[256,768]{1,0:T(8,128)(2,1)S(1)}) custom-call(bf16[256,768]{1,0:T(8,128)(2,1)S(1)} %collective-permute-done.16.n2.n2_oth, bf16[256,768]{1,0:T(8,128)(2,1)S(1)} %collective-permute-done.17.cot.cot_oth, bf16[768,768]{1,0:T(8,128)(2,1)S(1)} %copy-done.7, ...), custom_call_target="tpu_custom_call" | custom-call | flops 2000000000 | bytes 7477248 | tf_op jit(solution)/shard_map/mlp/pallas_call | solution.py:36
  118.4 3.4 %mlp_send.1 = bf16[2,768,768]{2,1,0:T(8,128)(2,1)} custom-call(s32[8]{0:T(128)S(1)} %stack.53.idx, bf16[256,1536]{1,0:T(8,128)(2,1)S(1)} %get-tuple-element.76.hid_own, bf16[256,1536]{1,0:T(8,128)(2,1)S(1)} %get-tuple-element.78.hid_oth, bf16[256,1536]{1,0:T(8,128)(2,1)S(1)} %get-tuple-element.103.gpre_own, ...), custom_call_target="tpu_custom_call" | custom-call | flops 2000000000 | bytes 7077920 | tf_op jit(solution)/shard_map/mlp_send/pallas_call | solution.py:36
  121.8 1.6 collective-permute-start.18
  123.4 10.0 %collective-permute-done.18.recv = bf16[256,768]{1,0:T(8,128)(2,1)S(1)} collective-permute-done((bf16[256,768]{1,0:T(8,128)(2,1)S(1)}, bf16[256,768]{1,0:T(8,128)(2,1)S(1)}, u32[]{:S(2)}, u32[]{:S(2)}) %collective-permute-start.18) | collective-permute-done | bytes 393248 | tf_op jit(solution)/shard_map/ppermute | solution.py:490
  134.1 1.6 collective-permute-start.19
  135.7 9.2 %collective-permute-done.19.gb_oth = bf16[256,768]{1,0:T(8,128)(2,1)S(1)} collective-permute-done((bf16[256,768]{1,0:T(8,128)(2,1)S(1)}, bf16[256,768]{1,0:T(8,128)(2,1)S(1)}, u32[]{:S(2)}, u32[]{:S(2)}) %collective-permute-start.19) | collective-permute-done | bytes 393248 | tf_op jit(solution)/shard_map/ppermute | solution.py:490
  144.9 3.5 %grad_mixed.1 = (bf16[512,768]{1,0:T(8,128)(2,1)S(1)}, bf16[6,512,128]{2,1,0:T(8,128)(2,1)S(1)}, bf16[416,128]{1,0:T(8,128)(2,1)S(1)}) custom-call(s32[8]{0:T(128)S(1)} %stack.53.idx, s32[1024]{0:T(1024)S(1)} %bitcast.68, bf16[256,768]{1,0:T(8,128)(2,1)S(1)} %get-tuple-element.83.gb_own, bf16[256,768]{1,0:T(8,128)(2,1)S(1)} %collective-permute-done.19.gb_oth, ...), custom_call_target="tpu_custom_call" | custom-call | flops 1000000000 | bytes 5421088 | tf_op jit(solution)/shard_map/grad_mixed/pallas_call | solution.py:36
  148.4 1.6 collective-permute-start.21
  150.0 1.9 down.1
  151.9 1.5 collective-permute-start.20
  154.0 1.3 collective-permute-start.24
  155.3 1.3 collective-permute-start.23
  156.6 1.3 collective-permute-start.22
  157.9 13.9 %inner_back.1 = (bf16[6,512,128]{2,1,0:T(8,128)(2,1)S(1)}, f32[6,512,128]{2,1,0:T(8,128)S(1)}, f32[6,512,128]{2,1,0:T(8,128)}) custom-call(s32[8]{0:T(128)S(1)} %stack.53.idx, s32[1024]{0:T(1024)S(1)} %bitcast.70, s32[512,1]{1,0:T(8,128)S(1)} %copy.41.segc, s32[1,512]{1,0:T(1,128)S(1)} %fusion.23.segr, bf16[6,512,128]{2,1,0:T(8,128)(2,1)S(1)} %get-tuple-element.65.fq, ...), custom_call_target="tpu_custom_call" | custom-call | flops 3000000000 | bytes 7282720 | tf_op jit(solution)/shard_map/inner_back/pallas_call | solution.py:36
  173.0 5.9 %qkv_back.1 = (bf16[6,512,128]{2,1,0:T(8,128)(2,1)S(1)}, bf16[512,1280]{1,0:T(8,128)(2,1)}, f32[256,768]{1,0:T(8,128)S(1)}, bf16[256,768]{1,0:T(8,128)(2,1)S(1)}) custom-call(s32[8]{0:T(128)S(1)} %stack.53.idx, s32[1024]{0:T(1024)S(1)} %bitcast.71, bf16[416,128]{1,0:T(8,128)(2,1)S(1)} %collective-permute-done.21.theirs, ...), custom_call_target="tpu_custom_call" | custom-call | flops 2000000000 | bytes 11376672 | tf_op jit(solution)/shard_map/qkv_back/pallas_call | solution.py:36
  180.2 5.0 %attn_weights.1 = (bf16[2,384,768]{2,1,0:T(8,128)(2,1)S(1)}, f32[2,384,768]{2,1,0:T(8,128)}, f32[2,200,128]{2,1,0:T(8,128)S(1)}) custom-call(s32[8]{0:T(128)S(1)} %stack.53.idx, bf16[512,768]{1,0:T(8,128)(2,1)S(1)} %copy-done.32, bf16[512,1280]{1,0:T(8,128)(2,1)} %get-tuple-element.97.gproj, bf16[512,512]{1,0:T(8,128)(2,1)S(1)} %copy-done.26, ...), custom_call_target="tpu_custom_call" | custom-call | flops 2000000000 | bytes 9510944 | tf_op jit(solution)/shard_map/attn_weights/pallas_call | solution.py:36
  185.2 2.9 collective-permute-done.25.recv
  189.7 4.8 %mlp_keep.1 = (f32[768,768]{1,0:T(8,128)}, bf16[768,768]{1,0:T(8,128)(2,1)S(1)}, f32[2,8,128]{2,1,0:T(8,128)S(1)}) custom-call(s32[8]{0:T(128)S(1)} %stack.53.idx, bf16[256,1536]{1,0:T(8,128)(2,1)S(1)} %copy-done.10, bf16[256,1536]{1,0:T(8,128)(2,1)S(1)} %copy-done.13, bf16[256,1536]{1,0:T(8,128)(2,1)S(1)} %copy-done.28, bf16[256,1536]{1,0:T(8,128)(2,1)S(1)} %copy-done.30, ...), custom_call_target="tpu_custom_call" | custom-call | flops 2000000000 | bytes 10625056 | tf_op jit(solution)/shard_map/mlp_keep/pallas_call | solution.py:36
  199.2 1.3 collective-permute-start.33
  201.4 1.7 copy.38
  204.1 2.4 collective-permute-start.29
  206.6 10.3 %collective-permute-done.33 = bf16[384,768]{1,0:T(8,128)(2,1)} collective-permute-done((bf16[384,768]{1,0:T(8,128)(2,1)}, bf16[384,768]{1,0:T(8,128)(2,1)}, u32[]{:S(2)}, u32[]{:S(2)}) %collective-permute-start.33) | collective-permute-done | bytes 589856 | tf_op jit(solution)/shard_map/ppermute | solution.py:490
  218.1 4.0 %collective-permute-start.30 = (f32[244,128]{1,0:T(8,128)S(1)}, f32[244,128]{1,0:T(8,128)S(1)}, u32[]{:S(2)}, u32[]{:S(2)}) collective-permute-start(f32[244,128]{1,0:T(8,128)S(1)} %fusion.21), channel_id=1, source_target_pairs={{0,4},{2,6},{4,0},{6,2},{1,5},{3,7},{5,1},{7,3},{8,12},{10,14},{12... | collective-permute-start | bytes 374792 | tf_op jit(solution)/shard_map/ppermute | solution.py:490
  222.1 1.8 collective-permute-start.34
  223.9 2.0 collective-permute-done.30
  227.8 2.6 collective-permute-done.34
  231.2 1.5 collective-permute-start.35
  235.6 10.6 %collective-permute-done.35 = bf16[192,768]{1,0:T(8,128)(2,1)} collective-permute-done((bf16[192,768]{1,0:T(8,128)(2,1)}, bf16[192,768]{1,0:T(8,128)(2,1)}, u32[]{:S(2)}, u32[]{:S(2)}) %collective-permute-start.35) | collective-permute-done | bytes 294944 | tf_op jit(solution)/shard_map/ppermute | solution.py:490
  247.4 1.5 convert_add_fusion
  249.0 2.1 collective-permute-start.43
  251.9 5.4 %collective-permute-done.36 = bf16[192,768]{1,0:T(8,128)(2,1)S(1)} collective-permute-done((bf16[192,768]{1,0:T(8,128)(2,1)S(1)}, bf16[192,768]{1,0:T(8,128)(2,1)S(1)}, u32[]{:S(2)}, u32[]{:S(2)}) %collective-permute-start.36) | collective-permute-done | bytes 294944 | tf_op jit(solution)/shard_map/ppermute | solution.py:490
  257.3 6.3 %collective-permute-done.43 = bf16[192,768]{1,0:T(8,128)(2,1)S(1)} collective-permute-done((bf16[192,768]{1,0:T(8,128)(2,1)S(1)}, bf16[192,768]{1,0:T(8,128)(2,1)S(1)}, u32[]{:S(2)}, u32[]{:S(2)}) %collective-permute-start.43) | collective-permute-done | bytes 294944 | tf_op jit(solution)/shard_map/ppermute | solution.py:490
  263.6 5.2 %collective-permute-done.39 = bf16[192,768]{1,0:T(8,128)(2,1)S(1)} collective-permute-done((bf16[192,768]{1,0:T(8,128)(2,1)S(1)}, bf16[192,768]{1,0:T(8,128)(2,1)S(1)}, u32[]{:S(2)}, u32[]{:S(2)}) %collective-permute-start.39) | collective-permute-done | bytes 294944 | tf_op jit(solution)/shard_map/ppermute | solution.py:490
  269.6 2.6 collective-permute-start.40
  272.8 17.9 %collective-permute-done.44 = bf16[192,768]{1,0:T(8,128)(2,1)S(1)} collective-permute-done((bf16[192,768]{1,0:T(8,128)(2,1)S(1)}, bf16[192,768]{1,0:T(8,128)(2,1)S(1)}, u32[]{:S(2)}, u32[]{:S(2)}) %collective-permute-start.44) | collective-permute-done | bytes 294944 | tf_op jit(solution)/shard_map/ppermute | solution.py:490
  290.8 6.1 %collective-permute-done.40 = bf16[192,768]{1,0:T(8,128)(2,1)S(1)} collective-permute-done((bf16[192,768]{1,0:T(8,128)(2,1)S(1)}, bf16[192,768]{1,0:T(8,128)(2,1)S(1)}, u32[]{:S(2)}, u32[]{:S(2)}) %collective-permute-start.40) | collective-permute-done | bytes 294944 | tf_op jit(solution)/shard_map/ppermute | solution.py:490
  297.4 12.1 %collective-permute-done.41 = bf16[192,768]{1,0:T(8,128)(2,1)S(1)} collective-permute-done((bf16[192,768]{1,0:T(8,128)(2,1)S(1)}, bf16[192,768]{1,0:T(8,128)(2,1)S(1)}, u32[]{:S(2)}, u32[]{:S(2)}) %collective-permute-start.41) | collective-permute-done | bytes 294944 | tf_op jit(solution)/shard_map/ppermute | solution.py:490
  311.3 1.3 pad_maximum_fusion
  312.9 1.6 maximum_convert_fusion
  314.7 1.6 maximum_convert_fusion.1
  (248 shorter events, 39.4 us)
Async XLA Ops:
  0.6 14.5 %copy-start.6 = (bf16[192,768]{1,0:T(8,128)(2,1)S(1)}, bf16[192,768]{1,0:T(8,128)(2,1)}, u32[]{:S(2)}) copy-start(bf16[192,768]{1,0:T(8,128)(2,1)} %w_own.3) | copy-start | bytes 884740
  1.9 13.2 %collective-permute-start.1 = (bf16[288,768]{1,0:T(8,128)(2,1)S(1)}, bf16[288,768]{1,0:T(8,128)(2,1)S(1)}, u32[]{:S(2)}, u32[]{:S(2)}) collective-permute-start(bf16[288,768]{1,0:T(8,128)(2,1)S(1)} %slice_select_fusion.2), channel_id=1, source_target_pairs={{0,16},{8,24},{16,0},{24,8},{1,17},{9,25},{17,1},{25,9},{2,18},{10... | collective-permute-start | bytes 1327112 | tf_op jit(solution)/shard_map/ppermute | solution.py:490
  15.1 1.8 collective-permute-start.2
  16.9 7.0 %copy-start.7 = (bf16[768,768]{1,0:T(8,128)(2,1)S(1)}, bf16[768,768]{1,0:T(8,128)(2,1)}, u32[]{:S(2)}) copy-start(bf16[768,768]{1,0:T(8,128)(2,1)} %up_own.3) | copy-start | bytes 3538948
  17.0 6.9 %copy-start.1 = (bf16[768,768]{1,0:T(8,128)(2,1)S(1)}, bf16[768,768]{1,0:T(8,128)(2,1)}, u32[]{:S(2)}) copy-start(bf16[768,768]{1,0:T(8,128)(2,1)} %down_own.5) | copy-start | bytes 3538948
  18.0 5.9 %collective-permute-start.9 = (bf16[96,768]{1,0:T(8,128)(2,1)S(1)}, bf16[96,768]{1,0:T(8,128)(2,1)S(1)}, u32[]{:S(2)}, u32[]{:S(2)}) collective-permute-start(bf16[96,768]{1,0:T(8,128)(2,1)S(1)} %slice_select_fusion.3), channel_id=1, source_target_pairs={{0,16},{8,24},{16,0},{24,8},{1,17},{9,25},{17,1},{25,9},{2,18},{10... | collective-permute-start | bytes 442376 | tf_op jit(solution)/shard_map/ppermute | solution.py:490
  23.9 1.4 collective-permute-start.10
  25.3 16.6 %collective-permute-start.12 = (bf16[384,768]{1,0:T(8,128)(2,1)}, bf16[384,768]{1,0:T(8,128)(2,1)}, u32[]{:S(2)}, u32[]{:S(2)}) collective-permute-start(bf16[384,768]{1,0:T(8,128)(2,1)} %get-tuple-element.74), channel_id=1, source_target_pairs={{0,16},{8,24},{16,0},{24,8},{1,17},{9,25},{17,1},{25,9},{2,18},{10... | collective-permute-start | bytes 1769480 | tf_op jit(solution)/shard_map/ppermute | solution.py:490
  27.3 14.5 %collective-permute-start.3 = (f32[1536]{0:T(1024)S(1)}, f32[1536]{0:T(1024)S(1)}, u32[]{:S(2)}, u32[]{:S(2)}) collective-permute-start(f32[1536]{0:T(1024)S(1)} %concatenate.61), channel_id=1, source_target_pairs={{0,16},{8,24},{16,0},{24,8},{1,17},{9,25},{17,1},{25,9},{2,18},{10... | collective-permute-start | bytes 18440 | tf_op jit(solution)/shard_map/ppermute | solution.py:490
  27.7 14.7 %collective-permute-start.4 = (bf16[3,64,64]{2,1,0:T(8,128)(2,1)S(1)}, bf16[3,64,64]{2,1,0:T(8,128)(2,1)S(1)}, u32[]{:S(2)}, u32[]{:S(2)}) collective-permute-start(bf16[3,64,64]{2,1,0:T(8,128)(2,1)S(1)} %copy-done.43), channel_id=1, source_target_pairs={{0,16},{8,24},{16,0},{24,8},{1,17},{9,25},{17,1},{25,9},{2,18},{10... | collective-permute-start | bytes 73736 | tf_op jit(solution)/shard_map/ppermute | solution.py:490
  29.7 18.7 %collective-permute-start = (bf16[256,768]{1,0:T(8,128)(2,1)S(1)}, bf16[256,768]{1,0:T(8,128)(2,1)S(1)}, u32[]{:S(2)}, u32[]{:S(2)}) collective-permute-start(bf16[256,768]{1,0:T(8,128)(2,1)S(1)} %ln_one.1.n_own), channel_id=1, source_target_pairs={{0,8},{8,0},{16,24},{24,16},{1,9},{9,1},{17,25},{25,17},{2,10},{10... | collective-permute-start | bytes 1179656 | tf_op jit(solution)/shard_map/ppermute | solution.py:490
  41.9 2.4 collective-permute-start.13
  46.7 27.8 %collective-permute-start.14 = (bf16[384,768]{1,0:T(8,128)(2,1)S(1)}, bf16[384,768]{1,0:T(8,128)(2,1)S(1)}, u32[]{:S(2)}, u32[]{:S(2)}) collective-permute-start(bf16[384,768]{1,0:T(8,128)(2,1)S(1)} %copy-done.42), channel_id=1, source_target_pairs={{0,16},{8,24},{16,0},{24,8},{1,17},{9,25},{17,1},{25,9},{2,18},{10... | collective-permute-start | bytes 1769480 | tf_op jit(solution)/shard_map/ppermute | solution.py:490
  55.1 9.2 %collective-permute-start.5 = (bf16[416,128]{1,0:T(8,128)(2,1)S(1)}, bf16[416,128]{1,0:T(8,128)(2,1)S(1)}, u32[]{:S(2)}, u32[]{:S(2)}) collective-permute-start(bf16[416,128]{1,0:T(8,128)(2,1)S(1)} %get-tuple-element.64.mine), channel_id=1, source_target_pairs={{0,16},{8,24},{16,0},{24,8},{1,17},{9,25},{17,1},{25,9},{2,18},{10... | collective-permute-start | bytes 319496 | tf_op jit(solution)/shard_map/ppermute | solution.py:490
  65.0 15.4 %collective-permute-start.8 = (bf16[416,128]{1,0:T(8,128)(2,1)S(1)}, bf16[416,128]{1,0:T(8,128)(2,1)S(1)}, u32[]{:S(2)}, u32[]{:S(2)}) collective-permute-start(bf16[416,128]{1,0:T(8,128)(2,1)S(1)} %state.1), channel_id=1, source_target_pairs={{0,6},{1,7},{8,14},{9,15},{16,22},{17,23},{24,30},{25,31}} | collective-permute-start | bytes 319496 | tf_op jit(solution)/shard_map/ppermute | solution.py:497
  70.7 9.7 %collective-permute-start.7 = (bf16[416,128]{1,0:T(8,128)(2,1)S(1)}, bf16[416,128]{1,0:T(8,128)(2,1)S(1)}, u32[]{:S(2)}, u32[]{:S(2)}) collective-permute-start(bf16[416,128]{1,0:T(8,128)(2,1)S(1)} %state.1), channel_id=1, source_target_pairs={{0,4},{2,6},{1,5},{3,7},{8,12},{10,14},{9,13},{11,15},{16,20},{18,... | collective-permute-start | bytes 319496 | tf_op jit(solution)/shard_map/ppermute | solution.py:497
  72.0 8.4 %collective-permute-start.6 = (bf16[416,128]{1,0:T(8,128)(2,1)S(1)}, bf16[416,128]{1,0:T(8,128)(2,1)S(1)}, u32[]{:S(2)}, u32[]{:S(2)}) collective-permute-start(bf16[416,128]{1,0:T(8,128)(2,1)S(1)} %state.1), channel_id=1, source_target_pairs={{0,2},{2,4},{4,6},{1,3},{3,5},{5,7},{8,10},{10,12},{12,14},{9,11},... | collective-permute-start | bytes 319496 | tf_op jit(solution)/shard_map/ppermute | solution.py:497
  74.5 24.5 %collective-permute-start.15 = (bf16[384,768]{1,0:T(8,128)(2,1)S(1)}, bf16[384,768]{1,0:T(8,128)(2,1)S(1)}, u32[]{:S(2)}, u32[]{:S(2)}) collective-permute-start(bf16[384,768]{1,0:T(8,128)(2,1)S(1)} %collective-permute-done.14), channel_id=1, source_target_pairs={{0,1},{1,0},{2,3},{3,2},{4,5},{5,4},{6,7},{7,6},{8,9},{9,8},{10,11... | collective-permute-start | bytes 1769480 | tf_op jit(solution)/shard_map/ppermute | solution.py:490
  80.4 6.3 %copy-start.14 = (bf16[256,1,768]{2,0,1:T(8,128)(2,1)S(1)}, bf16[256,1,768]{2,0,1:T(8,128)(2,1)}, u32[]{:S(2)}) copy-start(bf16[256,1,768]{2,0,1:T(8,128)(2,1)} %param.33) | copy-start | bytes 1179652
  85.1 11.9 %collective-permute-start.11 = (bf16[256,768]{1,0:T(8,128)(2,1)S(1)}, bf16[256,768]{1,0:T(8,128)(2,1)S(1)}, u32[]{:S(2)}, u32[]{:S(2)}) collective-permute-start(bf16[256,768]{1,0:T(8,128)(2,1)S(1)} %get-tuple-element.71), channel_id=1, source_target_pairs={{0,8},{8,0},{16,24},{24,16},{1,9},{9,1},{17,25},{25,17},{2,10},{10... | collective-permute-start | bytes 1179656 | tf_op jit(solution)/shard_map/ppermute | solution.py:490
  86.7 18.8 %collective-permute-start.17 = (bf16[256,768]{1,0:T(8,128)(2,1)S(1)}, bf16[256,768]{1,0:T(8,128)(2,1)S(1)}, u32[]{:S(2)}, u32[]{:S(2)}) collective-permute-start(bf16[256,768]{1,0:T(8,128)(2,1)S(1)} %bitcast.60), channel_id=1, source_target_pairs={{0,8},{8,0},{16,24},{24,16},{1,9},{9,1},{17,25},{25,17},{2,10},{10... | collective-permute-start | bytes 1179656 | tf_op jit(solution)/shard_map/ppermute | solution.py:490
  97.4 20.9 %copy-start.21 = (bf16[256,768]{1,0:T(8,128)(2,1)}, bf16[256,768]{1,0:T(8,128)(2,1)S(1)}, u32[]{:S(2)}) copy-start(bf16[256,768]{1,0:T(8,128)(2,1)S(1)} %get-tuple-element.73.n2.n2_own) | copy-start | bytes 1179652
  97.4 16.0 %collective-permute-start.16 = (bf16[256,768]{1,0:T(8,128)(2,1)S(1)}, bf16[256,768]{1,0:T(8,128)(2,1)S(1)}, u32[]{:S(2)}, u32[]{:S(2)}) collective-permute-start(bf16[256,768]{1,0:T(8,128)(2,1)S(1)} %get-tuple-element.73.n2.n2_own), channel_id=1, source_target_pairs={{0,8},{8,0},{16,24},{24,16},{1,9},{9,1},{17,25},{25,17},{2,10},{10... | collective-permute-start | bytes 1179656 | tf_op jit(solution)/shard_map/ppermute | solution.py:490
  104.9 13.5 %copy-start.8 = (bf16[256,1536]{1,0:T(8,128)(2,1)}, bf16[256,1536]{1,0:T(8,128)(2,1)S(1)}, u32[]{:S(2)}) copy-start(bf16[256,1536]{1,0:T(8,128)(2,1)S(1)} %get-tuple-element.76.hid_own) | copy-start | bytes 2359300
  104.9 13.5 %copy-start.27 = (bf16[256,1536]{1,0:T(8,128)(2,1)}, bf16[256,1536]{1,0:T(8,128)(2,1)S(1)}, u32[]{:S(2)}) copy-start(bf16[256,1536]{1,0:T(8,128)(2,1)S(1)} %get-tuple-element.103.gpre_own) | copy-start | bytes 2359300
  105.5 12.9 %copy-start.19 = (bf16[256,768]{1,0:T(8,128)(2,1)}, bf16[256,768]{1,0:T(8,128)(2,1)S(1)}, u32[]{:S(2)}) copy-start(bf16[256,768]{1,0:T(8,128)(2,1)S(1)} %collective-permute-done.17.cot.cot_oth) | copy-start | bytes 1179652
  121.8 66.9 %collective-permute-start.26 = (bf16[2,768,768]{2,1,0:T(8,128)(2,1)}, bf16[2,768,768]{2,1,0:T(8,128)(2,1)}, u32[]{:S(2)}, u32[]{:S(2)}) collective-permute-start(bf16[2,768,768]{2,1,0:T(8,128)(2,1)} %mlp_send.1), channel_id=1, source_target_pairs={{0,1},{1,0},{2,3},{3,2},{4,5},{5,4},{6,7},{7,6},{8,9},{9,8},{10,11... | collective-permute-start | bytes 7077896 | tf_op jit(solution)/shard_map/ppermute | solution.py:490
  121.8 11.5 %collective-permute-start.18 = (bf16[256,768]{1,0:T(8,128)(2,1)S(1)}, bf16[256,768]{1,0:T(8,128)(2,1)S(1)}, u32[]{:S(2)}, u32[]{:S(2)}) collective-permute-start(bf16[256,768]{1,0:T(8,128)(2,1)S(1)} %get-tuple-element.82), channel_id=1, source_target_pairs={{0,8},{8,0},{16,24},{24,16},{1,9},{9,1},{17,25},{25,17},{2,10},{10... | collective-permute-start | bytes 1179656 | tf_op jit(solution)/shard_map/ppermute | solution.py:490
  134.1 10.7 %collective-permute-start.19 = (bf16[256,768]{1,0:T(8,128)(2,1)S(1)}, bf16[256,768]{1,0:T(8,128)(2,1)S(1)}, u32[]{:S(2)}, u32[]{:S(2)}) collective-permute-start(bf16[256,768]{1,0:T(8,128)(2,1)S(1)} %get-tuple-element.83.gb_own), channel_id=1, source_target_pairs={{0,8},{8,0},{16,24},{24,16},{1,9},{9,1},{17,25},{25,17},{2,10},{10... | collective-permute-start | bytes 1179656 | tf_op jit(solution)/shard_map/ppermute | solution.py:490
  148.4 5.0 %collective-permute-start.21 = (bf16[416,128]{1,0:T(8,128)(2,1)S(1)}, bf16[416,128]{1,0:T(8,128)(2,1)S(1)}, u32[]{:S(2)}, u32[]{:S(2)}) collective-permute-start(bf16[416,128]{1,0:T(8,128)(2,1)S(1)} %get-tuple-element.86.mine), channel_id=1, source_target_pairs={{0,16},{8,24},{16,0},{24,8},{1,17},{9,25},{17,1},{25,9},{2,18},{10... | collective-permute-start | bytes 319496 | tf_op jit(solution)/shard_map/ppermute | solution.py:490
  151.9 48.6 %collective-permute-start.20 = (bf16[256,768]{1,0:T(8,128)(2,1)}, bf16[256,768]{1,0:T(8,128)(2,1)S(1)}, u32[]{:S(2)}, u32[]{:S(2)}) collective-permute-start(bf16[256,768]{1,0:T(8,128)(2,1)} %get-tuple-element.84), channel_id=1, source_target_pairs={{0,8},{8,0},{16,24},{24,16},{1,9},{9,1},{17,25},{25,17},{2,10},{10... | collective-permute-start | bytes 1179656 | tf_op jit(solution)/shard_map/ppermute | solution.py:490
  154.0 18.9 %collective-permute-start.24 = (bf16[416,128]{1,0:T(8,128)(2,1)S(1)}, bf16[416,128]{1,0:T(8,128)(2,1)S(1)}, u32[]{:S(2)}, u32[]{:S(2)}) collective-permute-start(bf16[416,128]{1,0:T(8,128)(2,1)S(1)} %gstate.1), channel_id=1, source_target_pairs={{6,0},{7,1},{14,8},{15,9},{22,16},{23,17},{30,24},{31,25}} | collective-permute-start | bytes 319496 | tf_op jit(solution)/shard_map/ppermute | solution.py:497
  155.3 17.6 %collective-permute-start.23 = (bf16[416,128]{1,0:T(8,128)(2,1)S(1)}, bf16[416,128]{1,0:T(8,128)(2,1)S(1)}, u32[]{:S(2)}, u32[]{:S(2)}) collective-permute-start(bf16[416,128]{1,0:T(8,128)(2,1)S(1)} %gstate.1), channel_id=1, source_target_pairs={{4,0},{6,2},{5,1},{7,3},{12,8},{14,10},{13,9},{15,11},{20,16},{22,... | collective-permute-start | bytes 319496 | tf_op jit(solution)/shard_map/ppermute | solution.py:497
  156.6 16.3 %collective-permute-start.22 = (bf16[416,128]{1,0:T(8,128)(2,1)S(1)}, bf16[416,128]{1,0:T(8,128)(2,1)S(1)}, u32[]{:S(2)}, u32[]{:S(2)}) collective-permute-start(bf16[416,128]{1,0:T(8,128)(2,1)S(1)} %gstate.1), channel_id=1, source_target_pairs={{2,0},{4,2},{6,4},{3,1},{5,3},{7,5},{10,8},{12,10},{14,12},{11,9},... | collective-permute-start | bytes 319496 | tf_op jit(solution)/shard_map/ppermute | solution.py:497
  173.0 7.2 %copy-start.26 = (bf16[512,512]{1,0:T(8,128)(2,1)S(1)}, bf16[512,512]{1,0:T(8,128)(2,1)}, u32[]{:S(2)}) copy-start(bf16[512,512]{1,0:T(8,128)(2,1)} %copy-done.25) | copy-start | bytes 1572868
  173.0 7.2 %copy-start.32 = (bf16[512,768]{1,0:T(8,128)(2,1)S(1)}, bf16[512,768]{1,0:T(8,128)(2,1)}, u32[]{:S(2)}) copy-start(bf16[512,768]{1,0:T(8,128)(2,1)} %copy-done.31) | copy-start | bytes 2359300
  173.0 7.2 %copy-start.34 = (bf16[512,768]{1,0:T(8,128)(2,1)S(1)}, bf16[512,768]{1,0:T(8,128)(2,1)}, u32[]{:S(2)}) copy-start(bf16[512,768]{1,0:T(8,128)(2,1)} %copy-done.33) | copy-start | bytes 2359300
  178.9 9.2 %collective-permute-start.25 = (bf16[256,768]{1,0:T(8,128)(2,1)S(1)}, bf16[256,768]{1,0:T(8,128)(2,1)S(1)}, u32[]{:S(2)}, u32[]{:S(2)}) collective-permute-start(bf16[256,768]{1,0:T(8,128)(2,1)S(1)} %get-tuple-element.93), channel_id=1, source_target_pairs={{0,8},{8,0},{16,24},{24,16},{1,9},{9,1},{17,25},{25,17},{2,10},{10... | collective-permute-start | bytes 1179656 | tf_op jit(solution)/shard_map/ppermute | solution.py:490
  180.2 8.6 %copy-start.22 = (bf16[256,768]{1,0:T(8,128)(2,1)S(1)}, bf16[256,768]{1,0:T(8,128)(2,1)}, u32[]{:S(2)}) copy-start(bf16[256,768]{1,0:T(8,128)(2,1)} %copy-done.21) | copy-start | bytes 1179652
  180.2 8.6 %copy-start.24 = (bf16[256,768]{1,0:T(8,128)(2,1)S(1)}, bf16[256,768]{1,0:T(8,128)(2,1)}, u32[]{:S(2)}) copy-start(bf16[256,768]{1,0:T(8,128)(2,1)} %copy-done.23) | copy-start | bytes 1179652
  180.2 8.6 %copy-start.28 = (bf16[256,1536]{1,0:T(8,128)(2,1)S(1)}, bf16[256,1536]{1,0:T(8,128)(2,1)}, u32[]{:S(2)}) copy-start(bf16[256,1536]{1,0:T(8,128)(2,1)} %copy-done.27) | copy-start | bytes 2359300
  180.2 8.6 %copy-start.30 = (bf16[256,1536]{1,0:T(8,128)(2,1)S(1)}, bf16[256,1536]{1,0:T(8,128)(2,1)}, u32[]{:S(2)}) copy-start(bf16[256,1536]{1,0:T(8,128)(2,1)} %copy-done.29) | copy-start | bytes 2359300
  185.2 9.4 %collective-permute-start.32 = (bf16[2,384,768]{2,1,0:T(8,128)(2,1)S(1)}, bf16[2,384,768]{2,1,0:T(8,128)(2,1)S(1)}, u32[]{:S(2)}, u32[]{:S(2)}) collective-permute-start(bf16[2,384,768]{2,1,0:T(8,128)(2,1)S(1)} %get-tuple-element.109), channel_id=1, source_target_pairs={{0,1},{1,0},{2,3},{3,2},{4,5},{5,4},{6,7},{7,6},{8,9},{9,8},{10,11... | collective-permute-start | bytes 3538952 | tf_op jit(solution)/shard_map/ppermute | solution.py:490
  194.5 1.6 collective-permute-start.27
  197.6 6.5 %collective-permute-start.28 = (f32[244,128]{1,0:T(8,128)}, f32[244,128]{1,0:T(8,128)S(1)}, u32[]{:S(2)}, u32[]{:S(2)}) collective-permute-start(f32[244,128]{1,0:T(8,128)} %slice.248), channel_id=1, source_target_pairs={{0,16},{8,24},{16,0},{24,8},{1,17},{9,25},{17,1},{25,9},{2,18},{10... | collective-permute-start | bytes 374792 | tf_op jit(solution)/shard_map/ppermute | solution.py:490
  199.2 17.7 %collective-permute-start.33 = (bf16[384,768]{1,0:T(8,128)(2,1)}, bf16[384,768]{1,0:T(8,128)(2,1)}, u32[]{:S(2)}, u32[]{:S(2)}) collective-permute-start(bf16[384,768]{1,0:T(8,128)(2,1)} %fusion.9), channel_id=1, source_target_pairs={{0,16},{8,24},{16,0},{24,8},{1,17},{9,25},{17,1},{25,9},{2,18},{10... | collective-permute-start | bytes 1769480 | tf_op jit(solution)/shard_map/ppermute | solution.py:490
  200.5 16.3 %copy-start.36 = (f32[2,384,768]{2,1,0:T(8,128)S(1)}, f32[2,384,768]{2,1,0:T(8,128)}, u32[]{:S(2)}) copy-start(f32[2,384,768]{2,1,0:T(8,128)} %copy-done.35) | copy-start | bytes 7077892
  203.1 44.3 %collective-permute-start.38 = (bf16[768,768]{1,0:T(8,128)(2,1)S(1)}, bf16[768,768]{1,0:T(8,128)(2,1)}, u32[]{:S(2)}, u32[]{:S(2)}) collective-permute-start(bf16[768,768]{1,0:T(8,128)(2,1)S(1)} %copy-done.18), channel_id=1, source_target_pairs={{0,16},{8,24},{16,0},{24,8},{1,17},{9,25},{17,1},{25,9},{2,18},{10... | collective-permute-start | bytes 3538952 | tf_op jit(solution)/shard_map/ppermute | solution.py:490
  204.1 13.9 %collective-permute-start.29 = (f32[244,128]{1,0:T(8,128)S(1)}, f32[244,128]{1,0:T(8,128)S(1)}, u32[]{:S(2)}, u32[]{:S(2)}) collective-permute-start(f32[244,128]{1,0:T(8,128)S(1)} %pad_maximum_fusion.9), channel_id=1, source_target_pairs={{0,2},{2,0},{4,6},{6,4},{1,3},{3,1},{5,7},{7,5},{8,10},{10,8},{12,... | collective-permute-start | bytes 374792 | tf_op jit(solution)/shard_map/ppermute | solution.py:490
  218.1 7.8 %collective-permute-start.30 = (f32[244,128]{1,0:T(8,128)S(1)}, f32[244,128]{1,0:T(8,128)S(1)}, u32[]{:S(2)}, u32[]{:S(2)}) collective-permute-start(f32[244,128]{1,0:T(8,128)S(1)} %fusion.21), channel_id=1, source_target_pairs={{0,4},{2,6},{4,0},{6,2},{1,5},{3,7},{5,1},{7,3},{8,12},{10,14},{12... | collective-permute-start | bytes 374792 | tf_op jit(solution)/shard_map/ppermute | solution.py:490
  222.1 8.3 %collective-permute-start.34 = (bf16[192,768]{1,0:T(8,128)(2,1)S(1)}, bf16[192,768]{1,0:T(8,128)(2,1)S(1)}, u32[]{:S(2)}, u32[]{:S(2)}) collective-permute-start(bf16[192,768]{1,0:T(8,128)(2,1)S(1)} %select_convert_fusion.4), channel_id=1, source_target_pairs={{0,2},{2,0},{4,6},{6,4},{1,3},{3,1},{5,7},{7,5},{8,10},{10,8},{12,... | collective-permute-start | bytes 884744 | tf_op jit(solution)/shard_map/ppermute | solution.py:490
  227.8 19.6 %copy-start.37 = (f32[768,768]{1,0:T(8,128)S(1)}, f32[768,768]{1,0:T(8,128)}, u32[]{:S(2)}) copy-start(f32[768,768]{1,0:T(8,128)} %get-tuple-element.110) | copy-start | bytes 7077892
  231.2 15.0 %collective-permute-start.35 = (bf16[192,768]{1,0:T(8,128)(2,1)}, bf16[192,768]{1,0:T(8,128)(2,1)}, u32[]{:S(2)}, u32[]{:S(2)}) collective-permute-start(bf16[192,768]{1,0:T(8,128)(2,1)} %add_convert_fusion.5), channel_id=1, source_target_pairs={{0,4},{2,6},{4,0},{6,2},{1,5},{3,7},{5,1},{7,3},{8,12},{10,14},{12... | collective-permute-start | bytes 884744 | tf_op jit(solution)/shard_map/ppermute | solution.py:490
  233.3 17.8 %collective-permute-start.31 = (f32[36,128]{1,0:T(8,128)}, f32[36,128]{1,0:T(8,128)S(1)}, u32[]{:S(2)}, u32[]{:S(2)}) collective-permute-start(f32[36,128]{1,0:T(8,128)} %slice.252), channel_id=1, source_target_pairs={{0,8},{8,0},{16,24},{24,16},{1,9},{9,1},{17,25},{25,17},{2,10},{10... | collective-permute-start | bytes 55304 | tf_op jit(solution)/shard_map/ppermute | solution.py:490
  247.3 10.0 %collective-permute-start.36 = (bf16[192,768]{1,0:T(8,128)(2,1)S(1)}, bf16[192,768]{1,0:T(8,128)(2,1)S(1)}, u32[]{:S(2)}, u32[]{:S(2)}) collective-permute-start(bf16[192,768]{1,0:T(8,128)(2,1)S(1)} %add_convert_fusion.4), channel_id=1, source_target_pairs={{0,2},{2,0},{4,6},{6,4},{1,3},{3,1},{5,7},{7,5},{8,10},{10,8},{12,... | collective-permute-start | bytes 884744 | tf_op jit(solution)/shard_map/ppermute | solution.py:490
  249.0 14.6 %collective-permute-start.43 = (bf16[192,768]{1,0:T(8,128)(2,1)S(1)}, bf16[192,768]{1,0:T(8,128)(2,1)S(1)}, u32[]{:S(2)}, u32[]{:S(2)}) collective-permute-start(bf16[192,768]{1,0:T(8,128)(2,1)S(1)} %get-tuple-element.146), channel_id=1, source_target_pairs={{0,2},{2,0},{4,6},{6,4},{1,3},{3,1},{5,7},{7,5},{8,10},{10,8},{12,... | collective-permute-start | bytes 884744 | tf_op jit(solution)/shard_map/ppermute | solution.py:490
  251.1 17.7 %collective-permute-start.39 = (bf16[192,768]{1,0:T(8,128)(2,1)S(1)}, bf16[192,768]{1,0:T(8,128)(2,1)S(1)}, u32[]{:S(2)}, u32[]{:S(2)}) collective-permute-start(bf16[192,768]{1,0:T(8,128)(2,1)S(1)} %get-tuple-element.147), channel_id=1, source_target_pairs={{0,2},{2,0},{4,6},{6,4},{1,3},{3,1},{5,7},{7,5},{8,10},{10,8},{12,... | collective-permute-start | bytes 884744 | tf_op jit(solution)/shard_map/ppermute | solution.py:490
  269.0 21.7 %collective-permute-start.44 = (bf16[192,768]{1,0:T(8,128)(2,1)S(1)}, bf16[192,768]{1,0:T(8,128)(2,1)S(1)}, u32[]{:S(2)}, u32[]{:S(2)}) collective-permute-start(bf16[192,768]{1,0:T(8,128)(2,1)S(1)} %get-tuple-element.144), channel_id=1, source_target_pairs={{0,4},{2,6},{4,0},{6,2},{1,5},{3,7},{5,1},{7,3},{8,12},{10,14},{12... | collective-permute-start | bytes 884744 | tf_op jit(solution)/shard_map/ppermute | solution.py:490
  269.5 27.6 %collective-permute-start.37 = (bf16[384,768]{1,0:T(8,128)(2,1)S(1)}, bf16[384,768]{1,0:T(8,128)(2,1)S(1)}, u32[]{:S(2)}, u32[]{:S(2)}) collective-permute-start(bf16[384,768]{1,0:T(8,128)(2,1)S(1)} %pad_maximum_fusion.4), channel_id=1, source_target_pairs={{0,1},{1,0},{2,3},{3,2},{4,5},{5,4},{6,7},{7,6},{8,9},{9,8},{10,11... | collective-permute-start | bytes 1769480 | tf_op jit(solution)/shard_map/ppermute | solution.py:490
  269.6 27.3 %collective-permute-start.40 = (bf16[192,768]{1,0:T(8,128)(2,1)S(1)}, bf16[192,768]{1,0:T(8,128)(2,1)S(1)}, u32[]{:S(2)}, u32[]{:S(2)}) collective-permute-start(bf16[192,768]{1,0:T(8,128)(2,1)S(1)} %get-tuple-element.145), channel_id=1, source_target_pairs={{0,4},{2,6},{4,0},{6,2},{1,5},{3,7},{5,1},{7,3},{8,12},{10,14},{12... | collective-permute-start | bytes 884744 | tf_op jit(solution)/shard_map/ppermute | solution.py:490
  290.7 19.9 %collective-permute-start.45 = (bf16[192,768]{1,0:T(8,128)(2,1)S(1)}, bf16[192,768]{1,0:T(8,128)(2,1)S(1)}, u32[]{:S(2)}, u32[]{:S(2)}) collective-permute-start(bf16[192,768]{1,0:T(8,128)(2,1)S(1)} %add_convert_fusion), channel_id=1, source_target_pairs={{0,2},{2,0},{4,6},{6,4},{1,3},{3,1},{5,7},{7,5},{8,10},{10,8},{12,... | collective-permute-start | bytes 884744 | tf_op jit(solution)/shard_map/ppermute | solution.py:490
  297.0 12.5 %collective-permute-start.41 = (bf16[192,768]{1,0:T(8,128)(2,1)S(1)}, bf16[192,768]{1,0:T(8,128)(2,1)S(1)}, u32[]{:S(2)}, u32[]{:S(2)}) collective-permute-start(bf16[192,768]{1,0:T(8,128)(2,1)S(1)} %add_convert_fusion.2), channel_id=1, source_target_pairs={{0,2},{2,0},{4,6},{6,4},{1,3},{3,1},{5,7},{7,5},{8,10},{10,8},{12,... | collective-permute-start | bytes 884744 | tf_op jit(solution)/shard_map/ppermute | solution.py:490
  309.6 3.1 collective-permute-start.42
  310.8 3.7 %collective-permute-start.46 = (bf16[384,768]{1,0:T(8,128)(2,1)S(1)}, bf16[384,768]{1,0:T(8,128)(2,1)S(1)}, u32[]{:S(2)}, u32[]{:S(2)}) collective-permute-start(bf16[384,768]{1,0:T(8,128)(2,1)S(1)} %pad_maximum_fusion.7), channel_id=1, source_target_pairs={{0,1},{1,0},{2,3},{3,2},{4,5},{5,4},{6,7},{7,6},{8,9},{9,8},{10,11... | collective-permute-start | bytes 1769480 | tf_op jit(solution)/shard_map/ppermute | solution.py:490
  (36 other events, 112.1 us)
